TPU v7x, 512 devices: a whole 4x8x8 slice. The times are simulated.
512 devices in a mesh: dom: 256 (over x, z, y), band: 2 (over core).
Axes of the slice: x: 4, y: 8, z: 8, core: 2. Of those that a mesh axis runs over, the one named last changes fastest.
Arguments:
- trial_block: float32 [32, 2048, 8, 128], P('band', 'dom'), may hold values from -18 to 18
- potential: float32 [2048, 8, 128], P('dom'), may hold values from -3 to 1
Outputs:
- orbitals: float32 [32, 2048, 8, 128], P('band', 'dom')
- projected: float32 [32, 32], replicated
All inputs are finite; a program needn't handle non-finite values.
Results may differ from a plain program's by a relative error of at most 0.0003.
Values sent between devices are 32-bit elements; how exact they have to be, the bound alone decides.
A program may use at most 64 MiB of HBM per device.

v0:
```python
import jax
import jax.numpy as jnp
from jax import lax
from jax.sharding import PartitionSpec as P

DEGREE = 4


COEFFS = (-205.0 / 72.0, 8.0 / 5.0, -1.0 / 5.0, 8.0 / 315.0, -1.0 / 560.0)
CENTER = 5.75
HALF_WIDTH = 5.25


def padded_2(block, sides, width):
    for axis, dim in sides:
        count = lax.axis_size(axis)
        forward = [(i, i + 1) for i in range(count - 1)]
        backward = [(target, source) for source, target in forward]
        low = lax.ppermute(
            lax.slice_in_dim(block, block.shape[dim] - width, None, axis=dim), axis, forward
        )
        high = lax.ppermute(lax.slice_in_dim(block, 0, width, axis=dim), axis, backward)
        block = jnp.concatenate([low, block, high], axis=dim)
    return block


def axis_second(field, axis):
    length = field.shape[axis]
    widths = [(0, 0)] * field.ndim
    widths[axis] = (4, 4)
    padded = jnp.pad(field, widths)
    summed = COEFFS[0] * field
    for offset in range(1, 5):
        upper = lax.slice_in_dim(padded, 4 + offset, 4 + offset + length, axis=axis)
        below = lax.slice_in_dim(padded, 4 - offset, 4 - offset + length, axis=axis)
        summed = summed + COEFFS[offset] * (upper + below)
    return summed


def hamiltonian(field, potential):
    extended = padded_2(field, (("dom", 1),), 4)
    length = field.shape[1]
    along = COEFFS[0] * field
    for offset in range(1, 5):
        along = along + COEFFS[offset] * (
            extended[:, 4 + offset : 4 + offset + length]
            + extended[:, 4 - offset : 4 - offset + length]
        )
    lap = along + axis_second(field, 2) + axis_second(field, 3)
    return -0.5 * lap + potential[None] * field


def chebyshev(start, potential):
    previous = start
    current = (hamiltonian(start, potential) - CENTER * start) / HALF_WIDTH
    for step in range(DEGREE - 1):
        following = (
            2.0 * (hamiltonian(current, potential) - CENTER * current) / HALF_WIDTH - previous
        )
        previous, current = (current, following)
    return current


def cell_product(left, right):
    return jnp.dot(left, right.T, precision=lax.Precision.HIGHEST)


def placed_block(block, band_first, bands):
    empty = jnp.zeros((bands, bands), jnp.float32)
    return lax.dynamic_update_slice(empty, block, (jnp.int32(0), band_first))


def spread(members, band_first, bands):
    widened = lax.all_gather(members[0], "band", axis=0, tiled=True)
    partials = tuple(
        (placed_block(cell_product(widened, member), band_first, bands) for member in members)
    )
    return (widened, partials)


def inverse_factor(gram):
    lower = jnp.linalg.cholesky(gram)
    identity = jnp.eye(gram.shape[0], dtype=jnp.float32)
    return lax.linalg.triangular_solve(lower, identity, left_side=True, lower=True)


def own_orbitals(ortho_wide, band_first, band_dev):
    return lax.dynamic_slice_in_dim(ortho_wide, band_first, band_dev, 0)


def shards(trial_block, potential):
    band_dev = trial_block.shape[0]
    block_shape = trial_block.shape
    filtered = chebyshev(trial_block, potential)
    flat = filtered.reshape(band_dev, -1)
    cell_count = flat.shape[1] * lax.axis_size("dom")
    bands = band_dev * lax.axis_size("band")
    band_first = lax.axis_index("band") * band_dev
    widened, partials = spread((flat,), band_first, bands)
    gram_total = lax.psum(partials[0], ("dom", "band"))
    inverse = inverse_factor(gram_total / cell_count)
    ortho_wide = jnp.dot(inverse, widened, precision=lax.Precision.HIGHEST)
    ortho_own = own_orbitals(ortho_wide, band_first, band_dev)
    image_own = hamiltonian(ortho_own.reshape(block_shape), potential).reshape(band_dev, -1)
    projection_part = placed_block(cell_product(ortho_wide, image_own), band_first, bands)
    projected = lax.psum(projection_part, ("dom", "band")) / cell_count
    return (ortho_own.reshape(block_shape), projected)


def solution(mesh):
    placed = (P("band", "dom", None, None), P("dom", None, None))
    return jax.shard_map(
        shards,
        mesh=mesh,
        in_specs=placed,
        out_specs=(P("band", "dom", None, None), P()),
        check_vma=False,
    )
```

profile of v0, /device:TPU:1, one launch (start us, length us, event | category | flops | bytes accessed | tf_op | source)
XLA Modules:
  0.0 329.8 jit_solution(13082815173536891150)
XLA Ops:
  8.3 4.2 %collective-permute-start.1 = (f32[16,4,8,128]{3,2,1,0:T(8,128)S(1)}, f32[16,4,8,128]{3,2,1,0:T(8,128)S(1)}, u32[]{:S(2)}, u32[]{:S(2)}) collective-permute-start(f32[16,4,8,128]{3,2,1,0:T(8,128)S(1)} %get-tuple-element.15), channel_id=1, source_target_pairs={{0,2},{2,4},{4,6},{6,8},{8,10},{10,12},{12,14},{14,16},{16,18},{18... | collective-permute-start | bytes 786440 | tf_op jit(solution)/shard_map/ppermute | solution.py:19
  12.5 1.3 collective-permute-start
  13.8 2.0 collective-permute-done.1
  15.9 3.7 %collective-permute-done = f32[16,4,8,128]{3,2,1,0:T(8,128)S(1)} collective-permute-done((f32[16,4,8,128]{3,2,1,0:T(8,128)S(1)}, f32[16,4,8,128]{3,2,1,0:T(8,128)S(1)}, u32[]{:S(2)}, u32[]{:S(2)}) %collective-permute-start) | collective-permute-done | bytes 262176 | tf_op jit(solution)/shard_map/ppermute | solution.py:22
  22.9 5.5 %collective-permute-start.3 = (f32[16,4,8,128]{3,2,1,0:T(8,128)S(1)}, f32[16,4,8,128]{3,2,1,0:T(8,128)S(1)}, u32[]{:S(2)}, u32[]{:S(2)}) collective-permute-start(f32[16,4,8,128]{3,2,1,0:T(8,128)S(1)} %get-tuple-element.13), channel_id=1, source_target_pairs={{0,2},{2,4},{4,6},{6,8},{8,10},{10,12},{12,14},{14,16},{16,18},{18... | collective-permute-start | bytes 786440 | tf_op jit(solution)/shard_map/ppermute | solution.py:19
  28.4 1.8 collective-permute-done.2
  30.2 1.5 collective-permute-done.3
  31.7 1.3 fusion.57
  34.3 6.0 %collective-permute-start.5 = (f32[16,4,8,128]{3,2,1,0:T(8,128)S(1)}, f32[16,4,8,128]{3,2,1,0:T(8,128)S(1)}, u32[]{:S(2)}, u32[]{:S(2)}) collective-permute-start(f32[16,4,8,128]{3,2,1,0:T(8,128)S(1)} %get-tuple-element.11), channel_id=1, source_target_pairs={{0,2},{2,4},{4,6},{6,8},{8,10},{10,12},{12,14},{14,16},{16,18},{18... | collective-permute-start | bytes 786440 | tf_op jit(solution)/shard_map/ppermute | solution.py:19
  40.3 1.8 collective-permute-done.4
  42.1 1.5 collective-permute-done.5
  43.6 1.3 fusion.34
  46.2 4.7 %collective-permute-start.7 = (f32[16,4,8,128]{3,2,1,0:T(8,128)S(1)}, f32[16,4,8,128]{3,2,1,0:T(8,128)S(1)}, u32[]{:S(2)}, u32[]{:S(2)}) collective-permute-start(f32[16,4,8,128]{3,2,1,0:T(8,128)S(1)} %get-tuple-element.9), channel_id=1, source_target_pairs={{0,2},{2,4},{4,6},{6,8},{8,10},{10,12},{12,14},{14,16},{16,18},{18... | collective-permute-start | bytes 786440 | tf_op jit(solution)/shard_map/ppermute | solution.py:19
  51.0 1.8 collective-permute-done.6
  52.8 1.5 collective-permute-done.7
  56.7 41.2 %all-gather.2.cloned.1.call-done = f32[32,8192]{1,0:T(8,128)} async-done(((f32[16,8192]{1,0:T(8,128)}), f32[32,8192]{1,0:T(8,128)}) %all-gather.2.cloned.1.call-update) | async-done | bytes 1048592 | tf_op jit(solution)/shard_map/all_gather | solution.py:74
  97.9 2.5 fusion.227
  100.7 98.6 %psum.14 = f32[32,32]{1,0:T(8,128)S(1)} all-reduce(f32[32,32]{1,0:T(8,128)S(1)} %dynamic_update_slice.6), channel_id=1, replica_groups=mesh['dom'=256,'band'=2] {'dom','band'}, use_global_device_ids=true, to_apply=%region_0.1 | all-reduce | flops 1024 | bytes 8192 | tf_op jit(solution)/shard_map/psum | solution.py:100
  199.4 2.9 cholesky.16
  203.6 2.4 custom-call.6
  207.5 2.7 collective-permute-start.9
  211.5 3.6 %collective-permute-done.9 = f32[16,4,8,128]{3,2,1,0:T(8,128)S(1)} collective-permute-done((f32[16,4,8,128]{3,2,1,0:T(8,128)S(1)}, f32[16,4,8,128]{3,2,1,0:T(8,128)S(1)}, u32[]{:S(2)}, u32[]{:S(2)}) %collective-permute-start.9) | collective-permute-done | bytes 262176 | tf_op jit(solution)/shard_map/ppermute | solution.py:19
  215.3 3.7 %collective-permute-done.8 = f32[16,4,8,128]{3,2,1,0:T(8,128)S(1)} collective-permute-done((f32[16,4,8,128]{3,2,1,0:T(8,128)S(1)}, f32[16,4,8,128]{3,2,1,0:T(8,128)S(1)}, u32[]{:S(2)}, u32[]{:S(2)}) %collective-permute-start.8) | collective-permute-done | bytes 262176 | tf_op jit(solution)/shard_map/ppermute | solution.py:22
  221.8 100.6 %psum.15 = f32[32,32]{1,0:T(8,128)S(1)} all-reduce(f32[32,32]{1,0:T(8,128)S(1)} %dynamic_update_slice.7), channel_id=1, replica_groups=mesh['dom'=256,'band'=2] {'dom','band'}, use_global_device_ids=true, to_apply=%region_3.4 | all-reduce | flops 1024 | bytes 8192 | tf_op jit(solution)/shard_map/psum | solution.py:106
  (46 shorter events, 17.6 us)
Async XLA Ops:
  7.2 90.7 %all-gather.2.cloned.1.call-start = ((), (), s32[]{:S(2)}) async-start(), calls=%async_computation | async-start | bytes 1572864 | tf_op jit(solution)/shard_map/all_gather | solution.py:74
  8.3 7.5 %copy-start.1 = (f32[16,8,8,128]{3,2,1,0:T(8,128)S(1)}, f32[16,8,8,128]{3,2,1,0:T(8,128)}, u32[]{:S(2)}) copy-start(f32[16,8,8,128]{3,2,1,0:T(8,128)} %param.2) | copy-start | bytes 1572868
  8.3 7.5 %collective-permute-start.1 = (f32[16,4,8,128]{3,2,1,0:T(8,128)S(1)}, f32[16,4,8,128]{3,2,1,0:T(8,128)S(1)}, u32[]{:S(2)}, u32[]{:S(2)}) collective-permute-start(f32[16,4,8,128]{3,2,1,0:T(8,128)S(1)} %get-tuple-element.15), channel_id=1, source_target_pairs={{0,2},{2,4},{4,6},{6,8},{8,10},{10,12},{12,14},{14,16},{16,18},{18... | collective-permute-start | bytes 786440 | tf_op jit(solution)/shard_map/ppermute | solution.py:19
  12.5 7.1 %collective-permute-start = (f32[16,4,8,128]{3,2,1,0:T(8,128)S(1)}, f32[16,4,8,128]{3,2,1,0:T(8,128)S(1)}, u32[]{:S(2)}, u32[]{:S(2)}) collective-permute-start(f32[16,4,8,128]{3,2,1,0:T(8,128)S(1)} %get-tuple-element.14), channel_id=1, source_target_pairs={{2,0},{4,2},{6,4},{8,6},{10,8},{12,10},{14,12},{16,14},{18,16},{20... | collective-permute-start | bytes 786440 | tf_op jit(solution)/shard_map/ppermute | solution.py:22
  19.6 0.8 copy-start.3
  21.6 8.6 %collective-permute-start.2 = (f32[16,4,8,128]{3,2,1,0:T(8,128)S(1)}, f32[16,4,8,128]{3,2,1,0:T(8,128)S(1)}, u32[]{:S(2)}, u32[]{:S(2)}) collective-permute-start(f32[16,4,8,128]{3,2,1,0:T(8,128)S(1)} %get-tuple-element.12), channel_id=1, source_target_pairs={{2,0},{4,2},{6,4},{8,6},{10,8},{12,10},{14,12},{16,14},{18,16},{20... | collective-permute-start | bytes 786440 | tf_op jit(solution)/shard_map/ppermute | solution.py:22
  22.9 8.8 %collective-permute-start.3 = (f32[16,4,8,128]{3,2,1,0:T(8,128)S(1)}, f32[16,4,8,128]{3,2,1,0:T(8,128)S(1)}, u32[]{:S(2)}, u32[]{:S(2)}) collective-permute-start(f32[16,4,8,128]{3,2,1,0:T(8,128)S(1)} %get-tuple-element.13), channel_id=1, source_target_pairs={{0,2},{2,4},{4,6},{6,8},{8,10},{10,12},{12,14},{14,16},{16,18},{18... | collective-permute-start | bytes 786440 | tf_op jit(solution)/shard_map/ppermute | solution.py:19
  33.0 9.1 %collective-permute-start.4 = (f32[16,4,8,128]{3,2,1,0:T(8,128)S(1)}, f32[16,4,8,128]{3,2,1,0:T(8,128)S(1)}, u32[]{:S(2)}, u32[]{:S(2)}) collective-permute-start(f32[16,4,8,128]{3,2,1,0:T(8,128)S(1)} %get-tuple-element.10), channel_id=1, source_target_pairs={{2,0},{4,2},{6,4},{8,6},{10,8},{12,10},{14,12},{16,14},{18,16},{20... | collective-permute-start | bytes 786440 | tf_op jit(solution)/shard_map/ppermute | solution.py:22
  34.3 9.2 %collective-permute-start.5 = (f32[16,4,8,128]{3,2,1,0:T(8,128)S(1)}, f32[16,4,8,128]{3,2,1,0:T(8,128)S(1)}, u32[]{:S(2)}, u32[]{:S(2)}) collective-permute-start(f32[16,4,8,128]{3,2,1,0:T(8,128)S(1)} %get-tuple-element.11), channel_id=1, source_target_pairs={{0,2},{2,4},{4,6},{6,8},{8,10},{10,12},{12,14},{14,16},{16,18},{18... | collective-permute-start | bytes 786440 | tf_op jit(solution)/shard_map/ppermute | solution.py:19
  44.9 7.9 %collective-permute-start.6 = (f32[16,4,8,128]{3,2,1,0:T(8,128)S(1)}, f32[16,4,8,128]{3,2,1,0:T(8,128)S(1)}, u32[]{:S(2)}, u32[]{:S(2)}) collective-permute-start(f32[16,4,8,128]{3,2,1,0:T(8,128)S(1)} %get-tuple-element.8), channel_id=1, source_target_pairs={{2,0},{4,2},{6,4},{8,6},{10,8},{12,10},{14,12},{16,14},{18,16},{20... | collective-permute-start | bytes 786440 | tf_op jit(solution)/shard_map/ppermute | solution.py:22
  46.2 8.0 %collective-permute-start.7 = (f32[16,4,8,128]{3,2,1,0:T(8,128)S(1)}, f32[16,4,8,128]{3,2,1,0:T(8,128)S(1)}, u32[]{:S(2)}, u32[]{:S(2)}) collective-permute-start(f32[16,4,8,128]{3,2,1,0:T(8,128)S(1)} %get-tuple-element.9), channel_id=1, source_target_pairs={{0,2},{2,4},{4,6},{6,8},{8,10},{10,12},{12,14},{14,16},{16,18},{18... | collective-permute-start | bytes 786440 | tf_op jit(solution)/shard_map/ppermute | solution.py:19
  97.9 108.4 %copy-start.2 = (f32[32,8192]{1,0:T(8,128)S(1)}, f32[32,8192]{1,0:T(8,128)}, u32[]{:S(2)}) copy-start(f32[32,8192]{1,0:T(8,128)} %all-gather.2.cloned.1.call-done) | copy-start | bytes 3145732
  207.5 11.5 %copy-start = (f32[2,8,64,128]{3,2,1,0:T(8,128)}, f32[2,8,64,128]{3,2,1,0:T(8,128)S(1)}, u32[]{:S(2)}) copy-start(f32[2,8,64,128]{3,2,1,0:T(8,128)S(1)} %copy.10) | copy-start | bytes 1572868
  207.5 7.6 %collective-permute-start.9 = (f32[16,4,8,128]{3,2,1,0:T(8,128)S(1)}, f32[16,4,8,128]{3,2,1,0:T(8,128)S(1)}, u32[]{:S(2)}, u32[]{:S(2)}) collective-permute-start(f32[16,4,8,128]{3,2,1,0:T(8,128)S(1)} %get-tuple-element.5), channel_id=1, source_target_pairs={{0,2},{2,4},{4,6},{6,8},{8,10},{10,12},{12,14},{14,16},{16,18},{18... | collective-permute-start | bytes 786440 | tf_op jit(solution)/shard_map/ppermute | solution.py:19
  210.2 8.8 %collective-permute-start.8 = (f32[16,4,8,128]{3,2,1,0:T(8,128)S(1)}, f32[16,4,8,128]{3,2,1,0:T(8,128)S(1)}, u32[]{:S(2)}, u32[]{:S(2)}) collective-permute-start(f32[16,4,8,128]{3,2,1,0:T(8,128)S(1)} %get-tuple-element.4), channel_id=1, source_target_pairs={{2,0},{4,2},{6,4},{8,6},{10,8},{12,10},{14,12},{16,14},{18,16},{20... | collective-permute-start | bytes 786440 | tf_op jit(solution)/shard_map/ppermute | solution.py:22
Sparse Core Ops, SparseCore 0:
  56.8 41.0 all-gather.1
where the time goes:
time: 330 us
  blocking collectives  199 us (60%)
  waiting for transfers between devices  64 us (19%)
  starting transfers between devices  29.5 us (9%)
  between operations  14.3 us (4%)
  other arithmetic  13.6 us (4%)
  matrix products  4.85 us (1%)
  local copies, waits for them, and re-layouts  4.3 us (1%)
    psum x1, blocking collectives, shards(): projected = lax.psum(projection_part, ('dom', 'band')) / cell_count  101 us
    psum x1, blocking collectives, shards(): gram_total = lax.psum(partials[0], ('dom', 'band'))  98.6 us
    all_gather x1, waiting for transfers between devices, spread(): widened = lax.all_gather(members[0], 'band', axis=0, tiled=True)  41.2 us
    ppermute x5, starting transfers between devices, padded_2(): lax.ppermute(lax.slice_in_dim(block, block.shape[dim] - width, None, axis...  23 us
    ppermute x5, waiting for transfers between devices, padded_2(): lax.ppermute(lax.slice_in_dim(block, 0, width, axis=dim), axis, backward)  12.8 us
    ppermute x5, waiting for transfers between devices, padded_2(): lax.ppermute(lax.slice_in_dim(block, block.shape[dim] - width, None, axis...  10.1 us
  transfers between devices with their start and end apart: 11, of which 11 were waited for; matrix products, arithmetic and copies ran while one was open for 0% of the time, Pallas kernels for 0%

commit v1 on v0

v1 whole, which is shorter than its diff:
```python
import functools

import jax
import jax.numpy as jnp
from jax import lax
from jax.experimental import pallas as pl
from jax.experimental.pallas import tpu as pltpu
from jax.sharding import PartitionSpec as P

COEFFS = (-205.0 / 72.0, 8.0 / 5.0, -1.0 / 5.0, 8.0 / 315.0, -1.0 / 560.0)
CENTER = 5.75
HALF_WIDTH = 5.25
DEGREE = 4

PAIR = tuple(-0.5 * c / HALF_WIDTH for c in COEFFS)
DIAG = -1.5 * COEFFS[0] - CENTER

MESH = pl.DeviceIdType.MESH
NT = (((1,), (1,)), ((), ()))
NN = (((1,), (0,)), ((), ()))
RINGS = {256: (4, 8, 8), 8: (2, 2, 2)}


def far_first(count):
    return sorted(range(1, count), key=lambda d: -min(d, count - d))


def kernel(
    rings,
    trial,
    potential,
    orbitals,
    projected,
    nat,
    pot,
    weight,
    field,
    halo,
    other,
    split,
    usplit,
    tile,
    slots,
    in_sem,
    halo_send,
    halo_recv,
    sib_send,
    sib_recv,
    red_send,
    red_recv,
):
    nx, nz, ny = rings
    doms = nx * nz * ny
    cells = doms * 8 * 8 * 128
    dom = lax.axis_index("dom")
    band = lax.axis_index("band")
    py = lax.rem(dom, ny)
    pz = lax.rem(lax.div(dom, ny), nz)
    px = lax.div(dom, ny * nz)
    left = lax.rem(dom + doms - 1, doms)
    right = lax.rem(dom + 1, doms)

    def at(x, z, y):
        return (x * nz + z) * ny + y

    def member_y(p):
        return {"dom": at(px, pz, p), "band": band}

    def member_z(p):
        return {"dom": at(px, p, py), "band": band}

    def member_x(p):
        return {"dom": at(lax.div(p, 2), pz, py), "band": lax.rem(p, 2)}

    phases = ((ny, py, member_y), (nz, pz, member_z), (2 * nx, 2 * px + band, member_x))

    loads = [
        pltpu.make_async_copy(potential, pot, in_sem.at[2]),
        pltpu.make_async_copy(trial.at[pl.ds(0, 512)], nat.at[pl.ds(0, 512)], in_sem.at[0]),
        pltpu.make_async_copy(trial.at[pl.ds(512, 512)], nat.at[pl.ds(512, 512)], in_sem.at[1]),
    ]
    for load in loads:
        load.start()

    barrier = pltpu.get_barrier_semaphore()
    greeted = 0
    for count, place, member in phases:
        for d in far_first(count):
            pl.semaphore_signal(
                barrier, inc=1, device_id=member(lax.rem(place + d, count)), device_id_type=MESH
            )
            greeted += 1
    for neighbour in (left, right):
        pl.semaphore_signal(
            barrier, inc=1, device_id={"dom": neighbour, "band": band}, device_id_type=MESH
        )
        greeted += 1

    zeros = jnp.zeros((4, 8, 8, 128), jnp.float32)

    def clear(i, carry):
        s, g = lax.div(i, 2), lax.rem(i, 2)
        field[s, g, pl.ds(0, 4)] = zeros
        field[s, g, pl.ds(12, 4)] = zeros
        return carry

    lax.fori_loop(0, 2 * (DEGREE + 1), clear, 0)

    loads[0].wait()

    def set_weight(x, carry):
        rows = (pot[x] + DIAG) * (1.0 / HALF_WIDTH)
        for y in range(8):
            weight[x, y] = jnp.broadcast_to(rows[y : y + 1], (8, 128))
        return carry

    lax.fori_loop(0, 8, set_weight, 0)

    def relayout(g):
        def body(x, carry):
            for y in range(8):
                field[0, g, 4 + x, y] = nat[pl.ds(g * 512 + x * 8 + y, 8, stride=64), :]
            return carry

        lax.fori_loop(0, 8, body, 0)

    def halo_copy(s, g, side):
        width = 4 if s < DEGREE else 2
        first = 12 - width if side == 0 else 4
        land = 4 - width if side == 0 else 0
        return pltpu.make_async_remote_copy(
            src_ref=field.at[s, g, pl.ds(first, width)],
            dst_ref=halo.at[s, g, side, pl.ds(land, width)],
            send_sem=halo_send.at[s, g, side],
            recv_sem=halo_recv.at[s, g, side],
            device_id={"dom": right if side == 0 else left, "band": band},
            device_id_type=MESH,
        )

    lane = lax.broadcasted_iota(jnp.int32, (8, 8, 128), 2)

    def shifted_y(c, k):
        empty = jnp.zeros((k, 8, 128), jnp.float32)
        return jnp.concatenate([c[k:], empty], 0) + jnp.concatenate([empty, c[: 8 - k]], 0)

    def shifted_z(c, k):
        below = jnp.where(lane >= k, pltpu.roll(c, k, 2), 0.0)
        return below + jnp.where(lane < 128 - k, pltpu.roll(c, 128 - k, 2), 0.0)

    def local_part(s, g):
        def body(x, carry):
            c = field[s, g, 4 + x]
            total = weight[x] * c
            for k in range(1, 5):
                pairs = field[s, g, 4 + x + k] + field[s, g, 4 + x - k]
                pairs = pairs + shifted_y(c, k) + shifted_z(c, k)
                total = total + PAIR[k] * pairs
            if 1 <= s < DEGREE:
                total = 2.0 * total - field[s - 1, g, 4 + x]
            field[s + 1, g, 4 + x] = total
            return carry

        lax.fori_loop(0, 8, body, 0)

    def halo_part(s, g, side):
        twice = 1.0 if s == 0 else 2.0
        for x in range(4):
            mine = 4 + x if side == 0 else 11 - x
            total = field[s + 1, g, mine]
            for layer in range(1, 5 - x):
                if s == DEGREE and (layer > 2 or (side == 1 and x < 2)):
                    continue
                theirs = 4 - layer if side == 0 else layer - 1
                total = total + (twice * PAIR[x + layer]) * halo[s, g, side, theirs]
            field[s + 1, g, mine] = total

    def add_halo(s, g, side):
        halo_copy(s, g, side).wait_recv()
        has = dom > 0 if side == 0 else dom < doms - 1

        @pl.when(has)
        def _():
            halo_part(s, g, side)

    def sibling_copy(g):
        return pltpu.make_async_remote_copy(
            src_ref=field.at[DEGREE, g, pl.ds(4, 8)],
            dst_ref=other.at[g],
            send_sem=sib_send.at[g],
            recv_sem=sib_recv.at[g],
            device_id={"dom": dom, "band": 1 - band},
            device_id_type=MESH,
        )

    def reduce_copy(m, f, d):
        count, place, member = phases[f]
        return pltpu.make_async_remote_copy(
            src_ref=slots.at[m, f, place],
            dst_ref=slots.at[m, f, place],
            send_sem=red_send.at[m, f, d],
            recv_sem=red_recv.at[m, f, place],
            device_id=member(lax.rem(place + d, count)),
            device_id_type=MESH,
        )

    def reduce_start(m, f, value):
        count, place, _ = phases[f]
        slots[m, f, place] = value
        for d in far_first(count):
            reduce_copy(m, f, d).start()

    def reduce_wait(m, f):
        count, place, member = phases[f]
        for d in range(1, count):
            source = lax.rem(place + d, count)
            pltpu.make_async_remote_copy(
                src_ref=slots.at[m, f, source],
                dst_ref=slots.at[m, f, source],
                send_sem=red_send.at[m, f, d],
                recv_sem=red_recv.at[m, f, source],
                device_id=member(source),
                device_id_type=MESH,
            ).wait_recv()

    def reduced(m, f):
        reduce_wait(m, f)
        total = slots[m, f, 0]
        for p in range(1, phases[f][0]):
            total = total + slots[m, f, p]
        return total

    def split_rows(value):
        high = value.astype(jnp.bfloat16)
        return high, (value - high.astype(jnp.float32)).astype(jnp.bfloat16)

    def split_own(target, s, first, low):
        def body(x, carry):
            for y in range(8):
                value = jnp.concatenate([field[s, 0, 4 + x, y], field[s, 1, 4 + x, y]], 0)
                hi, lo = split_rows(value)
                cols = pl.ds((y % 2) * 128, 128)
                target[x * 4 + y // 2, pl.ds(first, 16), cols] = hi
                target[x * 4 + y // 2, pl.ds(low + first, 16), cols] = lo
            return carry

        lax.fori_loop(0, 8, body, 0)

    def split_other(first):
        def body(x, carry):
            for y in range(8):
                hi, lo = split_rows(jnp.concatenate([other[0, x, y], other[1, x, y]], 0))
                cols = pl.ds((y % 2) * 128, 128)
                split[x * 4 + y // 2, pl.ds(first, 16), cols] = hi
                split[x * 4 + y // 2, pl.ds(32 + first, 16), cols] = lo
            return carry

        lax.fori_loop(0, 8, body, 0)

    own_rows = pl.multiple_of(band * 16, 16)
    other_rows = pl.multiple_of(16 - band * 16, 16)

    def products(left_of):
        def body(i, total):
            for j in range(4):
                total = total + lax.dot_general(
                    left_of(i * 4 + j), split[i * 4 + j], NT, preferred_element_type=jnp.float32
                )
            return total

        total = lax.fori_loop(0, 8, body, jnp.zeros((32, 64), jnp.float32))
        total = total[:16] + total[16:]
        tile[:, pl.ds(0, 64)] = total[:8]
        tile[:, pl.ds(64, 64)] = total[8:]
        return tile[...]

    def own_split(i):
        return jnp.concatenate(
            [split[i, pl.ds(own_rows, 16)], split[i, pl.ds(32 + own_rows, 16)]], 0
        )

    def unpacked(m):
        reduce_wait(m, 2)
        rows = []
        for core in range(2):
            total = slots[m, 2, core]
            for p in range(1, nx):
                total = total + slots[m, 2, 2 * p + core]
            total = total + pltpu.roll(total, 96, 1)
            rows += [total, pltpu.roll(total, 64, 1)]
        return rows

    pl.semaphore_wait(barrier, greeted)

    started = []

    def start(copy):
        copy.start()
        started.append(copy)

    for g in range(2):
        loads[1 + g].wait()
        relayout(g)
        for side in range(2):
            start(halo_copy(0, g, side))
    for g in range(2):
        local_part(0, g)
    for s in range(DEGREE):
        for g in range(2):
            for side in range(2):
                add_halo(s, g, side)
                if s + 1 < DEGREE:
                    start(halo_copy(s + 1, g, 1 - side))
            if s + 1 < DEGREE:
                local_part(s + 1, g)
            else:
                start(sibling_copy(g))
                for side in range(2):
                    start(halo_copy(DEGREE, g, side))

    split_own(split, DEGREE, own_rows, 32)
    for g in range(2):
        sibling_copy(g).wait_recv()
    split_other(other_rows)
    reduce_start(0, 0, products(own_split))
    for g in range(2):
        local_part(DEGREE, g)
    reduce_start(0, 1, reduced(0, 0))
    for g in range(2):
        for side in range(2):
            add_halo(DEGREE, g, side)
    split_own(usplit, DEGREE + 1, 0, 16)
    reduce_start(0, 2, reduced(0, 1))
    reduce_start(1, 0, products(lambda i: usplit[i]))

    lanes = lax.broadcasted_iota(jnp.int32, (8, 128), 1)
    subs = lax.broadcasted_iota(jnp.int32, (8, 128), 0)
    gram = [jnp.where(lanes < 32, r, 0.0) * (1.0 / cells) for r in unpacked(0)]
    rows = [
        jnp.where(lanes == subs + (32 + 8 * q), 1.0, gram[q]) for q in range(4)
    ]
    scale = [jnp.zeros((8, 128), jnp.float32) for _ in range(4)]
    for j in range(32):
        r, s = divmod(j, 8)
        row = jnp.broadcast_to(rows[r][s : s + 1], (8, 128))
        pivot = jnp.broadcast_to(row[:, j : j + 1], (8, 128))
        scale[r] = jnp.where(subs == s, pivot, scale[r])
        row = row / pivot
        for q in range(r, 4):
            new = rows[q] - jnp.broadcast_to(rows[q][:, j : j + 1], (8, 128)) * row
            rows[q] = jnp.where(subs > s, new, rows[q]) if q == r else new
    inverse = [
        jnp.where(lanes < 32, pltpu.roll(rows[q] * lax.rsqrt(scale[q]), 96, 1), 0.0)
        for q in range(4)
    ]

    own = [jnp.where(band == 0, inverse[q], inverse[2 + q]) for q in range(2)]
    own = jnp.concatenate([v + pltpu.roll(v, 32, 1) for v in own], 0)
    hi, lo = split_rows(own)
    own = jnp.concatenate([hi, lo], 0)[:, :64]

    def combine(x, carry):
        for y in range(0, 8, 2):
            value = lax.dot_general(
                own, split[x * 4 + y // 2], NN, preferred_element_type=jnp.float32
            )
            value = value[:16] + value[16:]
            nat[pl.ds(x * 8 + y, 16, stride=64), :] = value[:, :128]
            nat[pl.ds(x * 8 + y + 1, 16, stride=64), :] = value[:, 128:]
        return carry

    lax.fori_loop(0, 8, combine, 0)
    out = pltpu.make_async_copy(nat, orbitals, in_sem.at[0])
    out.start()

    reduce_start(1, 1, reduced(1, 0))
    reduce_start(1, 2, reduced(1, 1))
    image = [
        (HALF_WIDTH / cells) * i + CENTER * g for i, g in zip(unpacked(1), gram)
    ]
    image = jnp.concatenate(image, 0)[:, :32]
    inverse = jnp.concatenate(inverse, 0)[:, :32]
    dot = functools.partial(
        lax.dot_general, precision=lax.Precision.HIGHEST, preferred_element_type=jnp.float32
    )
    both = dot(inverse, image, NN) + dot(inverse, image, NT)
    projected[...] = 0.5 * dot(both, inverse, NT)

    for copy in started:
        copy.wait_send()
    for m in range(2):
        for f in range(3):
            for d in range(1, phases[f][0]):
                reduce_copy(m, f, d).wait_send()
    out.wait()


def shards(trial_block, potential):
    rings = RINGS[lax.axis_size("dom")]
    most = max(rings[1], rings[2], 2 * rings[0])
    f32, dma = jnp.float32, pltpu.SemaphoreType.DMA
    orbitals, projected = pl.pallas_call(
        functools.partial(kernel, rings),
        out_shape=(
            jax.ShapeDtypeStruct((1024, 128), f32),
            jax.ShapeDtypeStruct((32, 32), f32),
        ),
        in_specs=[pl.BlockSpec(memory_space=pl.ANY)] * 2,
        out_specs=(
            pl.BlockSpec(memory_space=pl.ANY),
            pl.BlockSpec(memory_space=pltpu.VMEM),
        ),
        scratch_shapes=[
            pltpu.VMEM((1024, 128), f32),
            pltpu.VMEM((8, 8, 128), f32),
            pltpu.VMEM((8, 8, 8, 128), f32),
            pltpu.VMEM((DEGREE + 2, 2, 16, 8, 8, 128), f32),
            pltpu.VMEM((DEGREE + 1, 2, 2, 4, 8, 8, 128), f32),
            pltpu.VMEM((2, 8, 8, 8, 128), f32),
            pltpu.VMEM((32, 64, 256), jnp.bfloat16),
            pltpu.VMEM((32, 32, 256), jnp.bfloat16),
            pltpu.VMEM((8, 128), f32),
            pltpu.VMEM((2, 3, most, 8, 128), f32),
            dma((3,)),
            dma((DEGREE + 1, 2, 2)),
            dma((DEGREE + 1, 2, 2)),
            dma((2,)),
            dma((2,)),
            dma((2, 3, most)),
            dma((2, 3, most)),
        ],
        compiler_params=pltpu.CompilerParams(
            collective_id=0, has_side_effects=True, vmem_limit_bytes=40 * 1024 * 1024
        ),
        cost_estimate=pl.CostEstimate(
            flops=200_000_000, bytes_accessed=1_100_000, transcendentals=0
        ),
    )(trial_block.reshape(1024, 128), potential)
    return orbitals.reshape(trial_block.shape), projected


def solution(mesh):
    return jax.shard_map(
        shards,
        mesh=mesh,
        in_specs=(P("band", "dom", None, None), P("dom", None, None)),
        out_specs=(P("band", "dom", None, None), P()),
        check_vma=False,
    )
```

time: 330 us -> 81.5 us (0.25)
  blocking collectives: 199 us -> 0 us
  Pallas kernels: 0 us -> 77.5 us
  waiting for transfers between devices: 64 us -> 0 us
  starting transfers between devices: 29.5 us -> 0 us
  between operations: 14.3 us -> 0.65 us
  other arithmetic: 13.6 us -> 0 us
  matrix products: 4.85 us -> 0 us
    psum x2 -> x0, blocking collectives: 199 us -> none  [the longest x1 101 us: shards(): projected = lax.psum(projection_part, ('dom', 'band')) / cell_count]
    pallas_call x0 -> x1, Pallas kernels: none -> 77.5 us  [shards(): pl.pallas_call(functools.partial(kernel, rings), out_shape=(jax.ShapeDtyp...]
    all_gather x1 -> x0, waiting for transfers between devices: 41.2 us -> none  [spread(): widened = lax.all_gather(members[0], 'band', axis=0, tiled=True)]
    ppermute x10 -> x0, starting transfers between devices: 29.5 us -> none  [the longest x5 23 us: padded_2(): lax.ppermute(lax.slice_in_dim(block, block.shape[dim] - width, None, axis...]
    ppermute x10 -> x0, waiting for transfers between devices: 22.8 us -> none  [the longest x5 12.8 us: padded_2(): lax.ppermute(lax.slice_in_dim(block, 0, width, axis=dim), axis, backward)]
    another operation x5 -> x0, other arithmetic: 6.68 us -> none  [the longest x3 3.59 us: inverse_factor(): lower = jnp.linalg.cholesky(gram)]
    dot_general x3 -> x0, matrix products: 4.63 us -> none  [the longest x2 3.62 us: cell_product(): return jnp.dot(left, right.T, precision=lax.Precision.HIGHEST)]
    sub x3 -> x0, other arithmetic: 3.9 us -> none  [chebyshev(): 2.0 * (hamiltonian(current, potential) - CENTER * current) / HALF_WIDTH]
  transfers between devices with their start and end apart: 11 -> 0, of which waited for: 11 -> 0; matrix products, arithmetic and copies ran while one was open for 0% -> 0% of each run, Pallas kernels for 0% -> 0%
where the time goes in v1:
time: 81.5 us; the launch traced here: 81.3 us
  Pallas kernels  77.5 us (95%)
  local copies, waits for them, and re-layouts  3.19 us (4%)
    pallas_call x1, Pallas kernels, shards(): pl.pallas_call(functools.partial(kernel, rings), out_shape=(jax.ShapeDtyp...  77.5 us
    unnamed x6, local copies, waits for them, and re-layouts  3.19 us

profile of v1, /device:TPU:1, one launch (start us, length us, event | category | flops | bytes accessed | tf_op | source)
XLA Modules:
  0.0 81.3 jit_solution(15127058724598056514)
XLA Ops:
  0.6 0.0 copy-start
  0.6 1.0 %copy-done = f32[16,8,8,128]{3,2,1,0:T(8,128)S(1)} copy-done((f32[16,8,8,128]{3,2,1,0:T(8,128)S(1)}, f32[16,8,8,128]{3,2,1,0:T(8,128)}, u32[]{:S(2)}) %copy-start) | copy-done | bytes 524312
  1.7 0.0 copy-start.1
  1.7 0.8 copy-done.1
  2.4 77.5 %shard_map.41 = (f32[1024,128]{1,0:T(8,128)S(1)}, f32[32,32]{1,0:T(8,128)S(1)}) custom-call(f32[1024,128]{1,0:T(8,128)S(1)} %bitcast.3, f32[8,8,128]{2,1,0:T(8,128)S(1)} %copy-done.1), custom_call_target="tpu_custom_call" | custom-call | flops 200000000 | bytes 1100000 | tf_op jit(solution)/shard_map/pallas_call | solution.py:401
  79.9 0.8 copy.6
  80.7 0.6 copy.7
Async XLA Ops:
  0.6 1.0 %copy-start = (f32[16,8,8,128]{3,2,1,0:T(8,128)S(1)}, f32[16,8,8,128]{3,2,1,0:T(8,128)}, u32[]{:S(2)}) copy-start(f32[16,8,8,128]{3,2,1,0:T(8,128)} %param.2) | copy-start | bytes 1572868
  1.7 0.8 copy-start.1

commit v2 on v1

v2 whole, which is shorter than its diff:
```python
import functools

import jax
import jax.numpy as jnp
from jax import lax
from jax.experimental import pallas as pl
from jax.experimental.pallas import tpu as pltpu
from jax.sharding import PartitionSpec as P

COEFFS = (-205.0 / 72.0, 8.0 / 5.0, -1.0 / 5.0, 8.0 / 315.0, -1.0 / 560.0)
CENTER = 5.75
HALF_WIDTH = 5.25
DEGREE = 4

PAIR = tuple(-0.5 * c / HALF_WIDTH for c in COEFFS)
DIAG = -1.5 * COEFFS[0] - CENTER

MESH = pl.DeviceIdType.MESH
NT = (((1,), (1,)), ((), ()))
NN = (((1,), (0,)), ((), ()))
PARTS = 4
YS = 8 // PARTS
SHIFT = (0, 8, 64, 72)
SUMS = ((0, 0), (0, 1), (1, 0), (1, 1), (1, 2))
RINGS = {256: (4, 8, 8), 8: (2, 2, 2)}


def far_first(count):
    return sorted(range(1, count), key=lambda d: -min(d, count - d))


def kernel(
    rings,
    trial,
    potential,
    orbitals,
    projected,
    nat,
    pot,
    pot_far,
    weight,
    weight_far,
    field,
    halo,
    far,
    other,
    split,
    usplit,
    tile,
    slots,
    in_sem,
    halo_send,
    halo_recv,
    far_send,
    far_recv,
    sib_send,
    sib_recv,
    red_send,
    red_recv,
):
    nx, nz, ny = rings
    doms = nx * nz * ny
    cells = doms * 8 * 8 * 128
    dom = lax.axis_index("dom")
    band = lax.axis_index("band")
    py = lax.rem(dom, ny)
    pz = lax.rem(lax.div(dom, ny), nz)
    px = lax.div(dom, ny * nz)
    left = lax.rem(dom + doms - 1, doms)
    right = lax.rem(dom + 1, doms)

    def at(x, z, y):
        return (x * nz + z) * ny + y

    pairs = nx // 2
    half = lax.div(px, 2)

    def member_yx(p):
        x = 2 * half + lax.rem(p, 2)
        return {"dom": at(x, pz, lax.div(p, 2)), "band": band}

    def member_zx(p):
        x = jnp.where(lax.rem(p, pairs) == half, px, nx - 1 - px)
        return {"dom": at(x, lax.div(p, pairs), py), "band": band}

    def member_core(p):
        return {"dom": dom, "band": p}

    phases = (
        (2 * ny, 2 * py + lax.rem(px, 2), member_yx),
        (pairs * nz, pairs * pz + half, member_zx),
        (2, band, member_core),
    )

    loads = [
        pltpu.make_async_copy(potential, pot, in_sem.at[2]),
        pltpu.make_async_copy(trial.at[pl.ds(0, 512)], nat.at[pl.ds(0, 512)], in_sem.at[0]),
        pltpu.make_async_copy(trial.at[pl.ds(512, 512)], nat.at[pl.ds(512, 512)], in_sem.at[1]),
    ]
    for load in loads:
        load.start()

    barrier = pltpu.get_barrier_semaphore()
    greeted = 0
    for count, place, member in phases:
        for d in far_first(count):
            pl.semaphore_signal(
                barrier, inc=1, device_id=member(lax.rem(place + d, count)), device_id_type=MESH
            )
            greeted += 1
    for neighbour in (left, right):
        pl.semaphore_signal(
            barrier, inc=1, device_id={"dom": neighbour, "band": band}, device_id_type=MESH
        )
        greeted += 1

    zeros = jnp.zeros((4, 8, 8, 128), jnp.float32)

    def clear(i, carry):
        s, g = lax.div(i, 2), lax.rem(i, 2)
        field[s, g, pl.ds(0, 4)] = zeros
        field[s, g, pl.ds(12, 4)] = zeros
        return carry

    def spread_weight(target, rows):
        rows = (rows + DIAG) * (1.0 / HALF_WIDTH)
        for y in range(8):
            target[y] = jnp.broadcast_to(rows[y : y + 1], (8, 128))

    def set_weight(x, carry):
        spread_weight(weight.at[x], pot[x])
        return carry

    def relayout(g):
        def body(x, carry):
            for y in range(8):
                field[0, g, 4 + x, y] = nat[pl.ds(g * 512 + x * 8 + y, 8, stride=64), :]
            return carry

        lax.fori_loop(0, 8, body, 0)

    has = (dom > 0, dom < doms - 1)

    def to_neighbour(side, src, dst, send_sem, recv_sem):
        return pltpu.make_async_remote_copy(
            src_ref=src,
            dst_ref=dst,
            send_sem=send_sem,
            recv_sem=recv_sem,
            device_id={"dom": right if side == 0 else left, "band": band},
            device_id_type=MESH,
        )

    def halo_copy(s, g, side, part):
        ys = pl.ds(part * YS, YS)
        return to_neighbour(
            side,
            field.at[s, g, pl.ds(8 if side == 0 else 4, 4), ys],
            halo.at[s, g, side, :, ys],
            halo_send.at[s, g, side, part],
            halo_recv.at[s, g, side, part],
        )

    def far_copy(g, side):
        return to_neighbour(
            side,
            field.at[last, g, pl.ds(6 if side == 0 else 8, 2)],
            far.at[g, side],
            far_send.at[g, side],
            far_recv.at[g, side],
        )

    def pot_copy(side):
        return to_neighbour(
            side,
            pot.at[pl.ds(6 if side == 0 else 0, 2)],
            pot_far.at[side],
            far_send.at[2, side],
            far_recv.at[2, side],
        )

    def send(side, copy):
        @pl.when(has[1 - side])
        def _():
            copy.start()

    lane = lax.broadcasted_iota(jnp.int32, (8, 8, 128), 2)

    def shifted_y(c, k):
        empty = jnp.zeros((k, 8, 128), jnp.float32)
        return jnp.concatenate([c[k:], empty], 0) + jnp.concatenate([empty, c[: 8 - k]], 0)

    def shifted_z(c, k):
        below = jnp.where(lane >= k, pltpu.roll(c, k, 2), 0.0)
        return below + jnp.where(lane < 128 - k, pltpu.roll(c, 128 - k, 2), 0.0)

    def local_part(s, g):
        def body(x, carry):
            c = field[s, g, 4 + x]
            total = weight[x] * c
            for k in range(1, 5):
                pairs = field[s, g, 4 + x + k] + field[s, g, 4 + x - k]
                pairs = pairs + shifted_y(c, k) + shifted_z(c, k)
                total = total + PAIR[k] * pairs
            if 1 <= s < DEGREE:
                total = 2.0 * total - field[s - 1, g, 4 + x]
            field[s + 1, g, 4 + x] = total
            return carry

        lax.fori_loop(0, 8, body, 0)

    def halo_part(s, g, side, part):
        twice = 1.0 if s == 0 else 2.0
        ys = pl.ds(part * YS, YS)
        layers = {n: halo[s, g, side, 4 - n if side == 0 else n - 1, ys] for n in range(1, 5)}
        for x in range(4):
            mine = 4 + x if side == 0 else 11 - x
            total = field[s + 1, g, mine, ys]
            for n in range(1, 5 - x):
                total = total + (twice * PAIR[x + n]) * layers[n]
            field[s + 1, g, mine, ys] = total

    def border_part(g, side):
        def cell(n):
            if n > 4:
                return far[g, side, 6 - n if side == 0 else n - 5]
            if n > 0:
                return halo[last, g, side, 4 - n if side == 0 else n - 1]
            return field[last, g, 4 - n if side == 0 else 11 + n]

        for n in (1, 2):
            c = cell(n)
            total = weight_far[side, 2 - n if side == 0 else n - 1] * c
            for k in range(1, 5):
                near = cell(n + k) + cell(n - k) + shifted_y(c, k) + shifted_z(c, k)
                total = total + PAIR[k] * near
            total = 2.0 * total - halo[last - 1, g, side, 4 - n if side == 0 else n - 1]
            for x in range(0 if side == 0 else 2, 5 - n):
                mine = 4 + x if side == 0 else 11 - x
                field[DEGREE + 1, g, mine] = field[DEGREE + 1, g, mine] + (2.0 * PAIR[x + n]) * total

    def sibling_copy(g, part):
        ys = pl.ds(part * YS, YS)
        return pltpu.make_async_remote_copy(
            src_ref=field.at[DEGREE, g, pl.ds(4, 8), ys],
            dst_ref=other.at[g, :, ys],
            send_sem=sib_send.at[g, part],
            recv_sem=sib_recv.at[g, part],
            device_id={"dom": dom, "band": 1 - band},
            device_id_type=MESH,
        )

    def reduce_copy(m, f, d):
        count, place, member = phases[f]
        return pltpu.make_async_remote_copy(
            src_ref=slots.at[m, f, place],
            dst_ref=slots.at[m, f, place],
            send_sem=red_send.at[m, f, d],
            recv_sem=red_recv.at[m, f, place],
            device_id=member(lax.rem(place + d, count)),
            device_id_type=MESH,
        )

    def reduce_start(m, f, value):
        count, place, _ = phases[f]
        slots[m, f, place] = value
        for d in far_first(count):
            reduce_copy(m, f, d).start()

    def reduce_wait(m, f):
        count, place, member = phases[f]
        for d in range(1, count):
            source = lax.rem(place + d, count)
            pltpu.make_async_remote_copy(
                src_ref=slots.at[m, f, source],
                dst_ref=slots.at[m, f, source],
                send_sem=red_send.at[m, f, d],
                recv_sem=red_recv.at[m, f, source],
                device_id=member(source),
                device_id_type=MESH,
            ).wait_recv()

    def reduced(m, f):
        reduce_wait(m, f)
        total = slots[m, f, 0]
        for p in range(1, phases[f][0]):
            total = total + slots[m, f, p]
        return total

    def split_rows(value):
        high = value.astype(jnp.bfloat16).astype(jnp.float32)
        return jnp.concatenate([high, value - high], 0).astype(jnp.bfloat16)

    def split_into(target, pair, first, read):
        def body(x, carry):
            both = [split_rows(read(x, 2 * pair + y)) for y in range(2)]
            target[x * 4 + pair, pl.ds(first, 16), :] = jnp.concatenate(both, 1)
            return carry

        lax.fori_loop(0, 8, body, 0, unroll=True)

    own_rows = pl.multiple_of(band * 32, 32)
    other_rows = pl.multiple_of(32 - band * 32, 32)

    def split_own(g, part):
        for pair in range(part * YS // 2, (part + 1) * YS // 2):
            split_into(split, pair, own_rows + 16 * g, lambda x, y: field[DEGREE, g, 4 + x, y])

    def split_other(g, part):
        for pair in range(part * YS // 2, (part + 1) * YS // 2):
            split_into(split, pair, other_rows + 16 * g, lambda x, y: other[g, x, y])

    def product(left, right):
        return lax.dot_general(left, right, NT, preferred_element_type=jnp.float32)

    def gram_part(part, total):
        for pair in range(part * YS // 2, (part + 1) * YS // 2):
            for x in range(8):
                total = total + product(split[x * 4 + pair], split[x * 4 + pair])
        return total

    def image_product():
        def body(x, total):
            for pair in range(4):
                total = total + product(usplit[x * 4 + pair], split[x * 4 + pair])
            return total

        return lax.fori_loop(0, 8, body, jnp.zeros((32, 64), jnp.float32))

    lanes = lax.broadcasted_iota(jnp.int32, (8, 128), 1)
    subs = lax.broadcasted_iota(jnp.int32, (8, 128), 0)
    used = (lanes < 64) & (lax.rem(lanes, 16) < 8)

    def folded(value):
        return value + pltpu.roll(value, 120, 1)

    def packed_gram(total):
        tile[:, pl.ds(0, 64)] = total
        value = jnp.zeros((8, 128), jnp.float32)
        for q in range(4):
            row = folded(tile[pl.ds(16 * q, 8)] + tile[pl.ds(16 * q + 8, 8)])
            row = jnp.where(used, row, 0.0)
            value = value + (row if q == 0 else pltpu.roll(row, SHIFT[q], 1))
        return value

    def unpacked_gram(value):
        rows = [value] + [pltpu.roll(value, 128 - SHIFT[q], 1) for q in range(1, 4)]
        return [jnp.where(used, row, 0.0) for row in rows]

    def packed_image(total):
        tile[pl.ds(0, 8), pl.ds(0, 64)] = total[:8] + total[8:16]
        tile[pl.ds(0, 8), pl.ds(64, 64)] = total[16:24] + total[24:]
        return tile[pl.ds(0, 8)]

    def unpacked_image():
        reduce_wait(1, 2)
        rows = []
        for core in range(2):
            total = folded(slots[1, 2, core])
            rows += [total, pltpu.roll(total, 64, 1)]
        return [jnp.where(used, row, 0.0) for row in rows]

    last = DEGREE - 1

    for g in range(2):
        loads[1 + g].wait()
        relayout(g)
        if g == 0:
            pl.semaphore_wait(barrier, greeted)
        for part in range(PARTS):
            for side in range(2):
                send(side, halo_copy(0, g, side, part))
    loads[0].wait()
    for side in range(2):
        send(side, pot_copy(side))
    lax.fori_loop(0, 2 * (DEGREE + 1), clear, 0)
    tile[...] = jnp.zeros((64, 128), jnp.float32)
    lax.fori_loop(0, 8, set_weight, 0)
    for g in range(2):
        local_part(0, g)

    for s in range(last):
        for g in range(2):

            def exchange(part, carry):
                for side in range(2):

                    @pl.when(has[side])
                    def _():
                        halo_copy(s, g, side, part).wait_recv()
                        halo_part(s, g, side, part)
                        halo_copy(s + 1, g, 1 - side, part).start()

                return carry

            lax.fori_loop(0, PARTS, exchange, 0)
            local_part(s + 1, g)
    for g in range(2):
        for side in range(2):
            send(side, far_copy(g, side))

    for side in range(2):

        @pl.when(has[side])
        def _():
            pot_copy(side).wait_recv()
            for n in range(2):
                spread_weight(weight_far.at[side, n], pot_far[side, n])

    gram = jnp.zeros((64, 64), jnp.float32)
    for g in range(2):
        for part in range(PARTS):
            for side in range(2):

                @pl.when(has[side])
                def _():
                    halo_copy(last, g, side, part).wait_recv()
                    halo_part(last, g, side, part)

            sibling_copy(g, part).start()
            split_own(g, part)
            if part > 0:
                sibling_copy(g, part - 1).wait_recv()
                split_other(g, part - 1)
                if g == 1:
                    gram = gram_part(part - 1, gram)
        if g == 0:
            local_part(DEGREE, 0)
        sibling_copy(g, PARTS - 1).wait_recv()
        split_other(g, PARTS - 1)
    reduce_start(0, 0, packed_gram(gram_part(PARTS - 1, gram)))

    local_part(DEGREE, 1)
    for side in range(2):

        @pl.when(has[side])
        def _():
            for g in range(2):
                far_copy(g, side).wait_recv()
                border_part(g, side)

    for g in range(2):
        for pair in range(4):
            split_into(usplit, pair, 16 * g, lambda x, y: field[DEGREE + 1, g, 4 + x, y])
    reduce_start(1, 0, packed_image(image_product()))
    reduce_start(0, 1, reduced(0, 0))
    reduce_start(1, 1, reduced(1, 0))

    gram = [row * (1.0 / cells) for row in unpacked_gram(reduced(0, 1))]
    rows = [jnp.where(lanes == subs + (64 + 16 * q), 1.0, gram[q]) for q in range(4)]
    inverse = eliminated(rows, subs)
    inverse = [jnp.where(used, pltpu.roll(row, 64, 1), 0.0) for row in inverse]

    reduce_start(1, 2, reduced(1, 1))
    own = [jnp.where(band == 0, inverse[q], inverse[2 + q]) for q in range(2)]
    own = split_rows(jnp.concatenate([v + pltpu.roll(v, 8, 1) for v in own], 0))[:, :64]

    def combine(x, carry):
        for y in range(0, 8, 2):
            value = lax.dot_general(
                own, split[x * 4 + y // 2], NN, preferred_element_type=jnp.float32
            )
            value = value[:16] + value[16:]
            nat[pl.ds(x * 8 + y, 16, stride=64), :] = value[:, :128]
            nat[pl.ds(x * 8 + y + 1, 16, stride=64), :] = value[:, 128:]
        return carry

    lax.fori_loop(0, 8, combine, 0)
    out = pltpu.make_async_copy(nat, orbitals, in_sem.at[0])
    out.start()

    dot = functools.partial(
        lax.dot_general, precision=lax.Precision.HIGHEST, preferred_element_type=jnp.float32
    )
    inverse = jnp.concatenate(inverse, 0)[:, :64]
    column = lax.broadcasted_iota(jnp.int32, (64, 32), 1)
    spread = lax.broadcasted_iota(jnp.int32, (64, 32), 0)
    spread = spread == 16 * lax.div(column, 8) + lax.rem(column, 8)
    narrow = dot(inverse, jnp.where(spread, 1.0, 0.0), NN)
    image = [(HALF_WIDTH / cells) * i + CENTER * g for i, g in zip(unpacked_image(), gram)]
    image = jnp.concatenate(image, 0)[:, :64]
    one = dot(dot(narrow, image, NN), inverse, NT)
    two = dot(dot(inverse, image, NT), narrow, NT)
    projected[...] = 0.5 * (one + two)

    for side in range(2):

        @pl.when(has[1 - side])
        def _():
            pot_copy(side).wait_send()
            for g in range(2):
                far_copy(g, side).wait_send()
                for s in range(DEGREE):
                    for part in range(PARTS):
                        halo_copy(s, g, side, part).wait_send()

    for g in range(2):
        for part in range(PARTS):
            sibling_copy(g, part).wait_send()
    for m, f in SUMS:
        for d in range(1, phases[f][0]):
            reduce_copy(m, f, d).wait_send()
    out.wait()


def eliminated(rows, subs):
    def spread(value):
        return jnp.broadcast_to(value, (8, 128))

    rows = list(rows)
    for r in range(4):
        lane = 16 * r
        column = {
            q: [spread(rows[q][:, lane + b : lane + b + 1]) for b in range(8)] for q in range(r, 4)
        }
        block = [[spread(column[r][b][a : a + 1]) for b in range(a + 1)] for a in range(8)]
        pivot = [spread(rows[r][a : a + 1]) for a in range(8)]
        factor = {q: [None] * 8 for q in range(r + 1, 4)}
        for k in range(8):
            reciprocal = 1.0 / block[k][k]
            for a in range(k + 1, 8):
                ratio = block[a][k] * reciprocal
                for b in range(k + 1, a + 1):
                    block[a][b] = block[a][b] - ratio * block[b][k]
                pivot[a] = pivot[a] - ratio * pivot[k]
            for q in range(r + 1, 4):
                factor[q][k] = column[q][k] * reciprocal
                for b in range(k + 1, 8):
                    column[q][b] = column[q][b] - factor[q][k] * block[b][k]
        for q in range(r + 1, 4):
            for k in range(8):
                rows[q] = rows[q] - factor[q][k] * pivot[k]
        done = pivot[0] * lax.rsqrt(block[0][0])
        for k in range(1, 8):
            done = jnp.where(subs == k, pivot[k] * lax.rsqrt(block[k][k]), done)
        rows[r] = done
    return rows


def shards(trial_block, potential):
    rings = RINGS[lax.axis_size("dom")]
    most = max(2 * rings[2], rings[0] // 2 * rings[1])
    f32, dma = jnp.float32, pltpu.SemaphoreType.DMA
    orbitals, projected = pl.pallas_call(
        functools.partial(kernel, rings),
        out_shape=(
            jax.ShapeDtypeStruct((1024, 128), f32),
            jax.ShapeDtypeStruct((32, 32), f32),
        ),
        in_specs=[pl.BlockSpec(memory_space=pl.ANY)] * 2,
        out_specs=(
            pl.BlockSpec(memory_space=pl.ANY),
            pl.BlockSpec(memory_space=pltpu.VMEM),
        ),
        scratch_shapes=[
            pltpu.VMEM((1024, 128), f32),
            pltpu.VMEM((8, 8, 128), f32),
            pltpu.VMEM((2, 2, 8, 128), f32),
            pltpu.VMEM((8, 8, 8, 128), f32),
            pltpu.VMEM((2, 2, 8, 8, 128), f32),
            pltpu.VMEM((DEGREE + 2, 2, 16, 8, 8, 128), f32),
            pltpu.VMEM((DEGREE, 2, 2, 4, 8, 8, 128), f32),
            pltpu.VMEM((2, 2, 2, 8, 8, 128), f32),
            pltpu.VMEM((2, 8, 8, 8, 128), f32),
            pltpu.VMEM((32, 64, 256), jnp.bfloat16),
            pltpu.VMEM((32, 32, 256), jnp.bfloat16),
            pltpu.VMEM((64, 128), f32),
            pltpu.VMEM((2, 3, most, 8, 128), f32),
            dma((3,)),
            dma((DEGREE, 2, 2, PARTS)),
            dma((DEGREE, 2, 2, PARTS)),
            dma((3, 2)),
            dma((3, 2)),
            dma((2, PARTS)),
            dma((2, PARTS)),
            dma((2, 3, most)),
            dma((2, 3, most)),
        ],
        compiler_params=pltpu.CompilerParams(
            collective_id=0, has_side_effects=True, vmem_limit_bytes=60 * 1024 * 1024
        ),
        cost_estimate=pl.CostEstimate(
            flops=200_000_000, bytes_accessed=1_100_000, transcendentals=0
        ),
    )(trial_block.reshape(1024, 128), potential)
    return orbitals.reshape(trial_block.shape), projected


def solution(mesh):
    return jax.shard_map(
        shards,
        mesh=mesh,
        in_specs=(P("band", "dom", None, None), P("dom", None, None)),
        out_specs=(P("band", "dom", None, None), P()),
        check_vma=False,
    )
```

time: 81.5 us -> 66.1 us (0.81)
  Pallas kernels: 77.5 us -> 62.8 us
    pallas_call x1, Pallas kernels: 77.5 us -> 62.8 us  [shards(): pl.pallas_call(functools.partial(kernel, rings), out_shape=(jax.ShapeDtyp...]
    unnamed x6 -> x4, local copies, waits for them, and re-layouts: 3.19 us -> 2.5 us
where the time goes in v2:
time: 66.1 us; the launch traced here: 65.9 us
  Pallas kernels  62.8 us (95%)
  local copies, waits for them, and re-layouts  2.5 us (4%)
    pallas_call x1, Pallas kernels, shards(): pl.pallas_call(functools.partial(kernel, rings), out_shape=(jax.ShapeDtyp...  62.8 us
    unnamed x4, local copies, waits for them, and re-layouts  2.5 us

profile of v2, /device:TPU:1, one launch (start us, length us, event | category | flops | bytes accessed | tf_op | source)
XLA Modules:
  0.0 65.9 jit_solution(8803919473301584527)
XLA Ops:
  0.6 62.8 %shard_map.41 = (f32[1024,128]{1,0:T(8,128)}, f32[32,32]{1,0:T(8,128)}) custom-call(f32[1024,128]{1,0:T(8,128)} %bitcast.3, f32[8,8,128]{2,1,0:T(8,128)} %potential.1), custom_call_target="tpu_custom_call" | custom-call | flops 200000000 | bytes 1100000 | tf_op jit(solution)/shard_map/pallas_call | solution.py:544
  63.4 0.0 copy-start
  63.4 1.9 %copy.6 = f32[16,8,8,128]{3,2,1,0:T(8,128)} copy(f32[16,8,8,128]{3,2,1,0:T(8,128)} %bitcast.2) | data formatting | bytes 1048576
  65.3 0.0 copy-done
  65.3 0.6 copy.7
Async XLA Ops:
  63.4 1.9 %copy-start = (f32[32,32]{1,0:T(8,128)S(1)}, f32[32,32]{1,0:T(8,128)}, u32[]{:S(2)}) copy-start(f32[32,32]{1,0:T(8,128)} %get-tuple-element.9) | copy-start | bytes 12292

commit v3 on v2

--- a/solution.py
+++ b/solution.py
@@ -18,10 +18,9 @@
 MESH = pl.DeviceIdType.MESH
 NT = (((1,), (1,)), ((), ()))
 NN = (((1,), (0,)), ((), ()))
-PARTS = 4
+PARTS = 2
 YS = 8 // PARTS
 SHIFT = (0, 8, 64, 72)
-SUMS = ((0, 0), (0, 1), (1, 0), (1, 1), (1, 2))
 RINGS = {256: (4, 8, 8), 8: (2, 2, 2)}
 
 
@@ -46,8 +45,11 @@
     other,
     split,
     usplit,
+    border,
+    weighted,
     tile,
     slots,
+    thin,
     in_sem,
     halo_send,
     halo_recv,
@@ -79,17 +81,20 @@
         x = 2 * half + lax.rem(p, 2)
         return {"dom": at(x, pz, lax.div(p, 2)), "band": band}
 
+    def member_core(p):
+        return {**member_yx(lax.div(p, 2)), "band": lax.rem(p, 2)}
+
     def member_zx(p):
         x = jnp.where(lax.rem(p, pairs) == half, px, nx - 1 - px)
         return {"dom": at(x, lax.div(p, pairs), py), "band": band}
 
-    def member_core(p):
-        return {"dom": dom, "band": p}
-
-    phases = (
-        (2 * ny, 2 * py + lax.rem(px, 2), member_yx),
-        (pairs * nz, pairs * pz + half, member_zx),
-        (2, band, member_core),
+    place_yx = 2 * py + lax.rem(px, 2)
+    along_z = (pairs * nz, pairs * pz + half, member_zx)
+    sums = (
+        (2 * ny, place_yx, member_yx, slots.at[0]),
+        (*along_z, slots.at[1]),
+        (4 * ny, 2 * place_yx + band, member_core, thin),
+        (*along_z, slots.at[2]),
     )
 
     loads = [
@@ -102,7 +107,7 @@
 
     barrier = pltpu.get_barrier_semaphore()
     greeted = 0
-    for count, place, member in phases:
+    for count, place, member, _ in sums[1:3]:
         for d in far_first(count):
             pl.semaphore_signal(
                 barrier, inc=1, device_id=member(lax.rem(place + d, count)), device_id_type=MESH
@@ -235,9 +240,7 @@
                 near = cell(n + k) + cell(n - k) + shifted_y(c, k) + shifted_z(c, k)
                 total = total + PAIR[k] * near
             total = 2.0 * total - halo[last - 1, g, side, 4 - n if side == 0 else n - 1]
-            for x in range(0 if side == 0 else 2, 5 - n):
-                mine = 4 + x if side == 0 else 11 - x
-                field[DEGREE + 1, g, mine] = field[DEGREE + 1, g, mine] + (2.0 * PAIR[x + n]) * total
+            split_layer(side, n, g, total)
 
     def sibling_copy(g, part):
         ys = pl.ds(part * YS, YS)
@@ -250,82 +253,102 @@
             device_id_type=MESH,
         )
 
-    def reduce_copy(m, f, d):
-        count, place, member = phases[f]
+    def sum_copy(f, d):
+        count, place, member, into = sums[f]
         return pltpu.make_async_remote_copy(
-            src_ref=slots.at[m, f, place],
-            dst_ref=slots.at[m, f, place],
-            send_sem=red_send.at[m, f, d],
-            recv_sem=red_recv.at[m, f, place],
+            src_ref=into.at[place],
+            dst_ref=into.at[place],
+            send_sem=red_send.at[f, d],
+            recv_sem=red_recv.at[f, place],
             device_id=member(lax.rem(place + d, count)),
             device_id_type=MESH,
         )
 
-    def reduce_start(m, f, value):
-        count, place, _ = phases[f]
-        slots[m, f, place] = value
+    def sum_start(f, value):
+        count, place, _, into = sums[f]
+        into[place] = value
         for d in far_first(count):
-            reduce_copy(m, f, d).start()
-
-    def reduce_wait(m, f):
-        count, place, member = phases[f]
+            sum_copy(f, d).start()
+
+    def summed(f):
+        count, place, member, into = sums[f]
         for d in range(1, count):
             source = lax.rem(place + d, count)
             pltpu.make_async_remote_copy(
-                src_ref=slots.at[m, f, source],
-                dst_ref=slots.at[m, f, source],
-                send_sem=red_send.at[m, f, d],
-                recv_sem=red_recv.at[m, f, source],
+                src_ref=into.at[source],
+                dst_ref=into.at[source],
+                send_sem=red_send.at[f, d],
+                recv_sem=red_recv.at[f, source],
                 device_id=member(source),
                 device_id_type=MESH,
             ).wait_recv()
-
-    def reduced(m, f):
-        reduce_wait(m, f)
-        total = slots[m, f, 0]
-        for p in range(1, phases[f][0]):
-            total = total + slots[m, f, p]
-        return total
+        step = 2 if f == 2 else 1
+        totals = []
+        for first in range(step):
+            total = into[first]
+            for p in range(first + step, count, step):
+                total = total + into[p]
+            totals.append(total)
+        return jnp.concatenate(totals, 0)
 
     def split_rows(value):
         high = value.astype(jnp.bfloat16).astype(jnp.float32)
         return jnp.concatenate([high, value - high], 0).astype(jnp.bfloat16)
 
-    def split_into(target, pair, first, read):
-        def body(x, carry):
-            both = [split_rows(read(x, 2 * pair + y)) for y in range(2)]
-            target[x * 4 + pair, pl.ds(first, 16), :] = jnp.concatenate(both, 1)
-            return carry
-
-        lax.fori_loop(0, 8, body, 0, unroll=True)
+    def lanes_at(x, y):
+        return pl.ds(128 * (8 * YS * (y // YS) + YS * x + y % YS), 128)
+
+    def split_into(target, first, ys, read):
+        for x in range(8):
+            for y in ys:
+                target[pl.ds(first, 16), lanes_at(x, y)] = split_rows(read(x, y))
 
     own_rows = pl.multiple_of(band * 32, 32)
     other_rows = pl.multiple_of(32 - band * 32, 32)
 
+    def of_part(part):
+        return range(part * YS, (part + 1) * YS)
+
     def split_own(g, part):
-        for pair in range(part * YS // 2, (part + 1) * YS // 2):
-            split_into(split, pair, own_rows + 16 * g, lambda x, y: field[DEGREE, g, 4 + x, y])
+        first = own_rows + 16 * g
+        split_into(split, first, of_part(part), lambda x, y: field[DEGREE, g, 4 + x, y])
 
     def split_other(g, part):
-        for pair in range(part * YS // 2, (part + 1) * YS // 2):
-            split_into(split, pair, other_rows + 16 * g, lambda x, y: other[g, x, y])
+        split_into(split, other_rows + 16 * g, of_part(part), lambda x, y: other[g, x, y])
 
     def product(left, right):
         return lax.dot_general(left, right, NT, preferred_element_type=jnp.float32)
 
     def gram_part(part, total):
-        for pair in range(part * YS // 2, (part + 1) * YS // 2):
-            for x in range(8):
-                total = total + product(split[x * 4 + pair], split[x * 4 + pair])
-        return total
-
-    def image_product():
-        def body(x, total):
-            for pair in range(4):
-                total = total + product(usplit[x * 4 + pair], split[x * 4 + pair])
-            return total
-
-        return lax.fori_loop(0, 8, body, jnp.zeros((32, 64), jnp.float32))
+        rows = split[:, pl.ds(part * YS * 1024, YS * 1024)]
+        return total + product(rows, rows)
+
+    def split_layer(side, n, g, value):
+        for y in range(8):
+            at_y = pl.ds(128 * (16 * side + 8 * n - 8 + y), 128)
+            border[pl.ds(16 * g, 16), at_y] = split_rows(value[y])
+
+    def weigh(first, read):
+        for side in range(2):
+            for n in (1, 2):
+                for y in range(8):
+                    total = None
+                    for x in range(0 if side == 0 else 2, 5 - n):
+                        value = (2.0 * PAIR[x + n]) * read(x if side == 0 else 7 - x, y)
+                        total = value if total is None else total + value
+                    at_y = pl.ds(128 * (16 * side + 8 * n - 8 + y), 128)
+                    weighted[pl.ds(first, 16), at_y] = split_rows(total)
+
+    def weigh_own(g):
+        weigh(own_rows + 16 * g, lambda x, y: field[DEGREE, g, 4 + x, y])
+
+    def weigh_other(g):
+        weigh(other_rows + 16 * g, lambda x, y: other[g, x, y])
+
+    def image_rows(g):
+        local_part(DEGREE, g)
+        split_into(usplit, 16 * g, range(8), lambda x, y: field[DEGREE + 1, g, 4 + x, y])
+        weigh_own(g)
 
     lanes = lax.broadcasted_iota(jnp.int32, (8, 128), 1)
     subs = lax.broadcasted_iota(jnp.int32, (8, 128), 0)
@@ -349,15 +372,16 @@
 
     def packed_image(total):
         tile[pl.ds(0, 8), pl.ds(0, 64)] = total[:8] + total[8:16]
-        tile[pl.ds(0, 8), pl.ds(64, 64)] = total[16:24] + total[24:]
-        return tile[pl.ds(0, 8)]
-
-    def unpacked_image():
-        reduce_wait(1, 2)
-        rows = []
-        for core in range(2):
-            total = folded(slots[1, 2, core])
-            rows += [total, pltpu.roll(total, 64, 1)]
+        tile[pl.ds(8, 8), pl.ds(0, 64)] = total[16:24] + total[24:]
+        one, two = [jnp.where(used, folded(tile[pl.ds(8 * g, 8)]), 0.0) for g in range(2)]
+        both = one + pltpu.roll(two, 8, 1)
+        return (both + pltpu.roll(pltpu.roll(both, 64, 1), 4, 0))[:4]
+
+    def unpacked_image(value):
+        moved = pltpu.roll(value, 64, 1)
+        one = jnp.where(subs < 4, value, pltpu.roll(moved, 4, 0))
+        two = jnp.where(subs < 4, pltpu.roll(value, 4, 0), moved)
+        rows = [one, pltpu.roll(one, 120, 1), two, pltpu.roll(two, 120, 1)]
         return [jnp.where(used, row, 0.0) for row in rows]
 
     last = DEGREE - 1
@@ -424,13 +448,15 @@
                 split_other(g, part - 1)
                 if g == 1:
                     gram = gram_part(part - 1, gram)
-        if g == 0:
-            local_part(DEGREE, 0)
+        image_rows(g)
         sibling_copy(g, PARTS - 1).wait_recv()
         split_other(g, PARTS - 1)
-    reduce_start(0, 0, packed_gram(gram_part(PARTS - 1, gram)))
-
-    local_part(DEGREE, 1)
+        if g == 0:
+            weigh_other(0)
+    sum_start(0, packed_gram(gram_part(PARTS - 1, gram)))
+
+    image = product(usplit[...], split[...])
+    weigh_other(1)
     for side in range(2):
 
         @pl.when(has[side])
@@ -439,33 +465,30 @@
                 far_copy(g, side).wait_recv()
                 border_part(g, side)
 
-    for g in range(2):
-        for pair in range(4):
-            split_into(usplit, pair, 16 * g, lambda x, y: field[DEGREE + 1, g, 4 + x, y])
-    reduce_start(1, 0, packed_image(image_product()))
-    reduce_start(0, 1, reduced(0, 0))
-    reduce_start(1, 1, reduced(1, 0))
-
-    gram = [row * (1.0 / cells) for row in unpacked_gram(reduced(0, 1))]
+        @pl.when(jnp.logical_not(has[side]))
+        def _():
+            border[:, pl.ds(2048 * side, 2048)] = jnp.zeros((32, 2048), jnp.bfloat16)
+
+    sum_start(2, packed_image(image + product(border[...], weighted[...])))
+    sum_start(1, summed(0))
+    sum_start(3, summed(2))
+
+    gram = [row * (1.0 / cells) for row in unpacked_gram(summed(1))]
     rows = [jnp.where(lanes == subs + (64 + 16 * q), 1.0, gram[q]) for q in range(4)]
     inverse = eliminated(rows, subs)
     inverse = [jnp.where(used, pltpu.roll(row, 64, 1), 0.0) for row in inverse]
 
-    reduce_start(1, 2, reduced(1, 1))
     own = [jnp.where(band == 0, inverse[q], inverse[2 + q]) for q in range(2)]
     own = split_rows(jnp.concatenate([v + pltpu.roll(v, 8, 1) for v in own], 0))[:, :64]
 
-    def combine(x, carry):
-        for y in range(0, 8, 2):
-            value = lax.dot_general(
-                own, split[x * 4 + y // 2], NN, preferred_element_type=jnp.float32
-            )
+    for part in range(PARTS):
+        for x in range(8):
+            at_x = pl.ds(128 * YS * (8 * part + x), 128 * YS)
+            value = lax.dot_general(own, split[:, at_x], NN, preferred_element_type=jnp.float32)
             value = value[:16] + value[16:]
-            nat[pl.ds(x * 8 + y, 16, stride=64), :] = value[:, :128]
-            nat[pl.ds(x * 8 + y + 1, 16, stride=64), :] = value[:, 128:]
-        return carry
-
-    lax.fori_loop(0, 8, combine, 0)
+            for y in range(YS):
+                row = x * 8 + part * YS + y
+                nat[pl.ds(row, 16, stride=64), :] = value[:, 128 * y : 128 * y + 128]
     out = pltpu.make_async_copy(nat, orbitals, in_sem.at[0])
     out.start()
 
@@ -477,7 +500,7 @@
     spread = lax.broadcasted_iota(jnp.int32, (64, 32), 0)
     spread = spread == 16 * lax.div(column, 8) + lax.rem(column, 8)
     narrow = dot(inverse, jnp.where(spread, 1.0, 0.0), NN)
-    image = [(HALF_WIDTH / cells) * i + CENTER * g for i, g in zip(unpacked_image(), gram)]
+    image = [(HALF_WIDTH / cells) * i + CENTER * g for i, g in zip(unpacked_image(summed(3)), gram)]
     image = jnp.concatenate(image, 0)[:, :64]
     one = dot(dot(narrow, image, NN), inverse, NT)
     two = dot(dot(inverse, image, NT), narrow, NT)
@@ -497,9 +520,9 @@
     for g in range(2):
         for part in range(PARTS):
             sibling_copy(g, part).wait_send()
-    for m, f in SUMS:
-        for d in range(1, phases[f][0]):
-            reduce_copy(m, f, d).wait_send()
+    for f in range(4):
+        for d in range(1, sums[f][0]):
+            sum_copy(f, d).wait_send()
     out.wait()
 
 
@@ -562,10 +585,13 @@
             pltpu.VMEM((DEGREE, 2, 2, 4, 8, 8, 128), f32),
             pltpu.VMEM((2, 2, 2, 8, 8, 128), f32),
             pltpu.VMEM((2, 8, 8, 8, 128), f32),
-            pltpu.VMEM((32, 64, 256), jnp.bfloat16),
-            pltpu.VMEM((32, 32, 256), jnp.bfloat16),
+            pltpu.VMEM((64, 8192), jnp.bfloat16),
+            pltpu.VMEM((32, 8192), jnp.bfloat16),
+            pltpu.VMEM((32, 4096), jnp.bfloat16),
+            pltpu.VMEM((64, 4096), jnp.bfloat16),
             pltpu.VMEM((64, 128), f32),
-            pltpu.VMEM((2, 3, most, 8, 128), f32),
+            pltpu.VMEM((3, most, 8, 128), f32),
+            pltpu.VMEM((4 * rings[2], 4, 128), f32),
             dma((3,)),
             dma((DEGREE, 2, 2, PARTS)),
             dma((DEGREE, 2, 2, PARTS)),
@@ -573,8 +599,8 @@
             dma((3, 2)),
             dma((2, PARTS)),
             dma((2, PARTS)),
-            dma((2, 3, most)),
-            dma((2, 3, most)),
+            dma((4, 4 * rings[2])),
+            dma((4, 4 * rings[2])),
         ],
         compiler_params=pltpu.CompilerParams(
             collective_id=0, has_side_effects=True, vmem_limit_bytes=60 * 1024 * 1024

time: 66.1 us -> 64.3 us (0.973)
  Pallas kernels: 62.8 us -> 61 us
    pallas_call x1, Pallas kernels: 62.8 us -> 61 us  [shards(): pl.pallas_call(functools.partial(kernel, rings), out_shape=(jax.ShapeDtyp...]
where the time goes in v3:
time: 64.3 us; the launch traced here: 64.2 us
  Pallas kernels  61 us (95%)
  local copies, waits for them, and re-layouts  2.5 us (4%)
  between operations  0.65 us (1%)
    pallas_call x1, Pallas kernels, shards(): pl.pallas_call(functools.partial(kernel, rings), out_shape=(jax.ShapeDtyp...  61 us
    unnamed x4, local copies, waits for them, and re-layouts  2.5 us

profile of v3, /device:TPU:1, one launch (start us, length us, event | category | flops | bytes accessed | tf_op | source)
XLA Modules:
  0.0 64.2 jit_solution(7422040660713063047)
XLA Ops:
  0.6 61.0 %shard_map.41 = (f32[1024,128]{1,0:T(8,128)}, f32[32,32]{1,0:T(8,128)}) custom-call(f32[1024,128]{1,0:T(8,128)} %bitcast.3, f32[8,8,128]{2,1,0:T(8,128)} %potential.1), custom_call_target="tpu_custom_call" | custom-call | flops 200000000 | bytes 1100000 | tf_op jit(solution)/shard_map/pallas_call | solution.py:567
  61.7 0.0 copy-start
  61.7 1.9 %copy.6 = f32[16,8,8,128]{3,2,1,0:T(8,128)} copy(f32[16,8,8,128]{3,2,1,0:T(8,128)} %bitcast.2) | data formatting | bytes 1048576
  63.6 0.0 copy-done
  63.6 0.6 copy.7
Async XLA Ops:
  61.7 1.9 %copy-start = (f32[32,32]{1,0:T(8,128)S(1)}, f32[32,32]{1,0:T(8,128)}, u32[]{:S(2)}) copy-start(f32[32,32]{1,0:T(8,128)} %get-tuple-element.9) | copy-start | bytes 12292

commit v4 on v3

--- a/solution.py
+++ b/solution.py
@@ -59,6 +59,7 @@
     sib_recv,
     red_send,
     red_recv,
+    known,
 ):
     nx, nz, ny = rings
     doms = nx * nz * ny
@@ -105,19 +106,36 @@
     for load in loads:
         load.start()
 
+    def along(axis, steps):
+        where = [px, pz, py]
+        size = rings[axis]
+        where[axis] = lax.rem(where[axis] + steps + size, size)
+        return {"dom": at(*where), "band": band}
+
+    one_hop = [along(axis, way) for axis in range(3) for way in (1, -1)]
+    two_hops = [
+        along(axis, way)
+        for axis in (1, 2)
+        for way in (2, -2)
+        if rings[axis] > 2
+    ]
+    sibling = {"dom": dom, "band": 1 - band}
+
     barrier = pltpu.get_barrier_semaphore()
-    greeted = 0
-    for count, place, member, _ in sums[1:3]:
-        for d in far_first(count):
+    nearest = one_hop + [{"dom": d, "band": band} for d in (left, right)] + [sibling]
+    for device in nearest:
+        pl.semaphore_signal(barrier, inc=1, device_id=device, device_id_type=MESH)
+    rounds = (one_hop, two_hops, two_hops, [sibling])
+
+    def tell(r):
+        for i, device in enumerate(rounds[r]):
             pl.semaphore_signal(
-                barrier, inc=1, device_id=member(lax.rem(place + d, count)), device_id_type=MESH
+                known.at[r, i], inc=1, device_id=device, device_id_type=MESH
             )
-            greeted += 1
-    for neighbour in (left, right):
-        pl.semaphore_signal(
-            barrier, inc=1, device_id={"dom": neighbour, "band": band}, device_id_type=MESH
-        )
-        greeted += 1
+
+    def hear(r):
+        for i in range(len(rounds[r])):
+            pl.semaphore_wait(known.at[r, i], 1)
 
     zeros = jnp.zeros((4, 8, 8, 128), jnp.float32)
 
@@ -390,10 +408,11 @@
         loads[1 + g].wait()
         relayout(g)
         if g == 0:
-            pl.semaphore_wait(barrier, greeted)
+            pl.semaphore_wait(barrier, len(nearest))
         for part in range(PARTS):
             for side in range(2):
                 send(side, halo_copy(0, g, side, part))
+    tell(0)
     loads[0].wait()
     for side in range(2):
         send(side, pot_copy(side))
@@ -419,6 +438,8 @@
 
             lax.fori_loop(0, PARTS, exchange, 0)
             local_part(s + 1, g)
+        hear(s)
+        tell(s + 1)
     for g in range(2):
         for side in range(2):
             send(side, far_copy(g, side))
@@ -453,6 +474,7 @@
         split_other(g, PARTS - 1)
         if g == 0:
             weigh_other(0)
+    hear(last)
     sum_start(0, packed_gram(gram_part(PARTS - 1, gram)))
 
     image = product(usplit[...], split[...])
@@ -601,6 +623,7 @@
             dma((2, PARTS)),
             dma((4, 4 * rings[2])),
             dma((4, 4 * rings[2])),
+            pltpu.SemaphoreType.REGULAR((4, 6)),
         ],
         compiler_params=pltpu.CompilerParams(
             collective_id=0, has_side_effects=True, vmem_limit_bytes=60 * 1024 * 1024

time: 64.3 us -> 62.9 us (0.978)
  Pallas kernels: 61 us -> 59.6 us
    pallas_call x1, Pallas kernels: 61 us -> 59.6 us  [shards(): pl.pallas_call(functools.partial(kernel, rings), out_shape=(jax.ShapeDtyp...]
where the time goes in v4:
time: 62.9 us; the launch traced here: 62.7 us
  Pallas kernels  59.6 us (95%)
  local copies, waits for them, and re-layouts  2.5 us (4%)
  between operations  0.65 us (1%)
    pallas_call x1, Pallas kernels, shards(): pl.pallas_call(functools.partial(kernel, rings), out_shape=(jax.ShapeDtyp...  59.6 us
    unnamed x4, local copies, waits for them, and re-layouts  2.5 us

profile of v4, /device:TPU:1, one launch (start us, length us, event | category | flops | bytes accessed | tf_op | source)
XLA Modules:
  0.0 62.7 jit_solution(10018046521303205546)
XLA Ops:
  0.6 59.6 %shard_map.41 = (f32[1024,128]{1,0:T(8,128)}, f32[32,32]{1,0:T(8,128)}) custom-call(f32[1024,128]{1,0:T(8,128)} %bitcast.3, f32[8,8,128]{2,1,0:T(8,128)} %potential.1), custom_call_target="tpu_custom_call" | custom-call | flops 200000000 | bytes 1100000 | tf_op jit(solution)/shard_map/pallas_call | solution.py:589
  60.2 0.0 copy-start
  60.2 1.9 %copy.6 = f32[16,8,8,128]{3,2,1,0:T(8,128)} copy(f32[16,8,8,128]{3,2,1,0:T(8,128)} %bitcast.2) | data formatting | bytes 1048576
  62.1 0.0 copy-done
  62.1 0.6 copy.7
Async XLA Ops:
  60.2 1.9 %copy-start = (f32[32,32]{1,0:T(8,128)S(1)}, f32[32,32]{1,0:T(8,128)}, u32[]{:S(2)}) copy-start(f32[32,32]{1,0:T(8,128)} %get-tuple-element.9) | copy-start | bytes 12292

commit v5 on v4

--- a/solution.py
+++ b/solution.py
@@ -42,6 +42,7 @@
     field,
     halo,
     far,
+    layers,
     other,
     split,
     usplit,
@@ -235,18 +236,16 @@
     def halo_part(s, g, side, part):
         twice = 1.0 if s == 0 else 2.0
         ys = pl.ds(part * YS, YS)
-        layers = {n: halo[s, g, side, 4 - n if side == 0 else n - 1, ys] for n in range(1, 5)}
+        cells_at = {n: halo[s, g, side, 4 - n if side == 0 else n - 1, ys] for n in range(1, 5)}
         for x in range(4):
             mine = 4 + x if side == 0 else 11 - x
             total = field[s + 1, g, mine, ys]
             for n in range(1, 5 - x):
-                total = total + (twice * PAIR[x + n]) * layers[n]
+                total = total + (twice * PAIR[x + n]) * cells_at[n]
             field[s + 1, g, mine, ys] = total
 
-    def border_part(g, side):
+    def border_start(g, side):
         def cell(n):
-            if n > 4:
-                return far[g, side, 6 - n if side == 0 else n - 5]
             if n > 0:
                 return halo[last, g, side, 4 - n if side == 0 else n - 1]
             return field[last, g, 4 - n if side == 0 else 11 + n]
@@ -255,10 +254,18 @@
             c = cell(n)
             total = weight_far[side, 2 - n if side == 0 else n - 1] * c
             for k in range(1, 5):
-                near = cell(n + k) + cell(n - k) + shifted_y(c, k) + shifted_z(c, k)
+                near = cell(n - k) + shifted_y(c, k) + shifted_z(c, k)
+                if n + k < 5:
+                    near = near + cell(n + k)
                 total = total + PAIR[k] * near
             total = 2.0 * total - halo[last - 1, g, side, 4 - n if side == 0 else n - 1]
-            split_layer(side, n, g, total)
+            layers[g, side, n - 1] = total
+
+    def border_end(g, side):
+        five, six = [far[g, side, 6 - n if side == 0 else n - 5] for n in (5, 6)]
+        split_layer(side, 1, g, layers[g, side, 0] + (2.0 * PAIR[4]) * five)
+        total = layers[g, side, 1] + (2.0 * PAIR[3]) * five
+        split_layer(side, 2, g, total + (2.0 * PAIR[4]) * six)
 
     def sibling_copy(g, part):
         ys = pl.ds(part * YS, YS)
@@ -276,8 +283,8 @@
         return pltpu.make_async_remote_copy(
             src_ref=into.at[place],
             dst_ref=into.at[place],
-            send_sem=red_send.at[f, d],
-            recv_sem=red_recv.at[f, place],
+            send_sem=red_send.at[f],
+            recv_sem=red_recv.at[f],
             device_id=member(lax.rem(place + d, count)),
             device_id_type=MESH,
         )
@@ -288,18 +295,21 @@
         for d in far_first(count):
             sum_copy(f, d).start()
 
+    def sum_tiles(f):
+        count, place, member, into = sums[f]
+        tiles = into.at[pl.ds(0, count - 1)]
+        return pltpu.make_async_remote_copy(
+            src_ref=tiles,
+            dst_ref=tiles,
+            send_sem=red_send.at[f],
+            recv_sem=red_recv.at[f],
+            device_id=member(lax.rem(place + 1, count)),
+            device_id_type=MESH,
+        )
+
     def summed(f):
-        count, place, member, into = sums[f]
-        for d in range(1, count):
-            source = lax.rem(place + d, count)
-            pltpu.make_async_remote_copy(
-                src_ref=into.at[source],
-                dst_ref=into.at[source],
-                send_sem=red_send.at[f, d],
-                recv_sem=red_recv.at[f, source],
-                device_id=member(source),
-                device_id_type=MESH,
-            ).wait_recv()
+        count, _, _, into = sums[f]
+        sum_tiles(f).wait_recv()
         step = 2 if f == 2 else 1
         totals = []
         for first in range(step):
@@ -367,6 +377,8 @@
         local_part(DEGREE, g)
         split_into(usplit, 16 * g, range(8), lambda x, y: field[DEGREE + 1, g, 4 + x, y])
         weigh_own(g)
+        for side in range(2):
+            pl.when(has[side])(functools.partial(border_start, g, side))
 
     lanes = lax.broadcasted_iota(jnp.int32, (8, 128), 1)
     subs = lax.broadcasted_iota(jnp.int32, (8, 128), 0)
@@ -479,13 +491,15 @@
 
     image = product(usplit[...], split[...])
     weigh_other(1)
+    for g in range(2):
+        for side in range(2):
+
+            @pl.when(has[side])
+            def _():
+                far_copy(g, side).wait_recv()
+                border_end(g, side)
+
     for side in range(2):
-
-        @pl.when(has[side])
-        def _():
-            for g in range(2):
-                far_copy(g, side).wait_recv()
-                border_part(g, side)
 
         @pl.when(jnp.logical_not(has[side]))
         def _():
@@ -522,12 +536,6 @@
     spread = lax.broadcasted_iota(jnp.int32, (64, 32), 0)
     spread = spread == 16 * lax.div(column, 8) + lax.rem(column, 8)
     narrow = dot(inverse, jnp.where(spread, 1.0, 0.0), NN)
-    image = [(HALF_WIDTH / cells) * i + CENTER * g for i, g in zip(unpacked_image(summed(3)), gram)]
-    image = jnp.concatenate(image, 0)[:, :64]
-    one = dot(dot(narrow, image, NN), inverse, NT)
-    two = dot(dot(inverse, image, NT), narrow, NT)
-    projected[...] = 0.5 * (one + two)
-
     for side in range(2):
 
         @pl.when(has[1 - side])
@@ -543,8 +551,14 @@
         for part in range(PARTS):
             sibling_copy(g, part).wait_send()
     for f in range(4):
-        for d in range(1, sums[f][0]):
-            sum_copy(f, d).wait_send()
+        sum_tiles(f).wait_send()
+
+    image = [(HALF_WIDTH / cells) * i + CENTER * g for i, g in zip(unpacked_image(summed(3)), gram)]
+    image = jnp.concatenate(image, 0)[:, :64]
+    one = dot(dot(narrow, image, NN), inverse, NT)
+    two = dot(dot(inverse, image, NT), narrow, NT)
+    projected[...] = 0.5 * (one + two)
+
     out.wait()
 
 
@@ -606,6 +620,7 @@
             pltpu.VMEM((DEGREE + 2, 2, 16, 8, 8, 128), f32),
             pltpu.VMEM((DEGREE, 2, 2, 4, 8, 8, 128), f32),
             pltpu.VMEM((2, 2, 2, 8, 8, 128), f32),
+            pltpu.VMEM((2, 2, 2, 8, 8, 128), f32),
             pltpu.VMEM((2, 8, 8, 8, 128), f32),
             pltpu.VMEM((64, 8192), jnp.bfloat16),
             pltpu.VMEM((32, 8192), jnp.bfloat16),
@@ -621,8 +636,8 @@
             dma((3, 2)),
             dma((2, PARTS)),
             dma((2, PARTS)),
-            dma((4, 4 * rings[2])),
-            dma((4, 4 * rings[2])),
+            dma((4,)),
+            dma((4,)),
             pltpu.SemaphoreType.REGULAR((4, 6)),
         ],
         compiler_params=pltpu.CompilerParams(

time: 62.9 us -> 60.8 us (0.967)
  Pallas kernels: 59.6 us -> 57.5 us
    pallas_call x1, Pallas kernels: 59.6 us -> 57.5 us  [shards(): pl.pallas_call(functools.partial(kernel, rings), out_shape=(jax.ShapeDtyp...]
where the time goes in v5:
time: 60.8 us; the launch traced here: 60.6 us
  Pallas kernels  57.5 us (95%)
  local copies, waits for them, and re-layouts  2.5 us (4%)
  between operations  0.65 us (1%)
    pallas_call x1, Pallas kernels, shards(): pl.pallas_call(functools.partial(kernel, rings), out_shape=(jax.ShapeDtyp...  57.5 us
    unnamed x4, local copies, waits for them, and re-layouts  2.5 us

profile of v5, /device:TPU:1, one launch (start us, length us, event | category | flops | bytes accessed | tf_op | source)
XLA Modules:
  0.0 60.6 jit_solution(8880293580895130114)
XLA Ops:
  0.6 57.5 %shard_map.41 = (f32[1024,128]{1,0:T(8,128)}, f32[32,32]{1,0:T(8,128)}) custom-call(f32[1024,128]{1,0:T(8,128)} %bitcast.3, f32[8,8,128]{2,1,0:T(8,128)} %potential.1), custom_call_target="tpu_custom_call" | custom-call | flops 200000000 | bytes 1100000 | tf_op jit(solution)/shard_map/pallas_call | solution.py:603
  58.1 0.0 copy-start
  58.1 1.9 %copy.6 = f32[16,8,8,128]{3,2,1,0:T(8,128)} copy(f32[16,8,8,128]{3,2,1,0:T(8,128)} %bitcast.2) | data formatting | bytes 1048576
  60.0 0.0 copy-done
  60.0 0.6 copy.7
Async XLA Ops:
  58.1 1.9 %copy-start = (f32[32,32]{1,0:T(8,128)S(1)}, f32[32,32]{1,0:T(8,128)}, u32[]{:S(2)}) copy-start(f32[32,32]{1,0:T(8,128)} %get-tuple-element.9) | copy-start | bytes 12292

commit v6 on v5

--- a/solution.py
+++ b/solution.py
@@ -21,6 +21,7 @@
 PARTS = 2
 YS = 8 // PARTS
 SHIFT = (0, 8, 64, 72)
+CHUNKS = 2
 RINGS = {256: (4, 8, 8), 8: (2, 2, 2)}
 
 
@@ -231,7 +232,7 @@
             field[s + 1, g, 4 + x] = total
             return carry
 
-        lax.fori_loop(0, 8, body, 0)
+        lax.fori_loop(0, 8, body, 0, unroll=True)
 
     def halo_part(s, g, side, part):
         twice = 1.0 if s == 0 else 2.0
@@ -419,8 +420,8 @@
     for g in range(2):
         loads[1 + g].wait()
         relayout(g)
-        if g == 0:
-            pl.semaphore_wait(barrier, len(nearest))
+    pl.semaphore_wait(barrier, len(nearest))
+    for g in range(2):
         for part in range(PARTS):
             for side in range(2):
                 send(side, halo_copy(0, g, side, part))
@@ -594,6 +595,22 @@
             done = jnp.where(subs == k, pivot[k] * lax.rsqrt(block[k][k]), done)
         rows[r] = done
     return rows
+
+
+def hand_over(orbitals, projected, orbitals_out, projected_out, rows, matrix, read_sem, write_sem):
+    steps = [(projected, matrix, projected_out)]
+    for i in range(CHUNKS):
+        part = pl.ds(i * (1024 // CHUNKS), 1024 // CHUNKS)
+        steps.append((orbitals.at[part], rows.at[part], orbitals_out.at[part]))
+    reads = [pltpu.make_async_copy(a, b, read_sem.at[i]) for i, (a, b, _) in enumerate(steps)]
+    writes = [pltpu.make_async_copy(b, c, write_sem.at[i]) for i, (_, b, c) in enumerate(steps)]
+    for read in reads:
+        read.start()
+    for read, write in zip(reads, writes):
+        read.wait()
+        write.start()
+    for write in writes:
+        write.wait()
 
 
 def shards(trial_block, potential):
@@ -647,6 +664,23 @@
             flops=200_000_000, bytes_accessed=1_100_000, transcendentals=0
         ),
     )(trial_block.reshape(1024, 128), potential)
+    anywhere = pl.BlockSpec(memory_space=pl.ANY)
+    orbitals, projected = pl.pallas_call(
+        hand_over,
+        out_shape=(
+            jax.ShapeDtypeStruct((1024, 128), f32),
+            jax.ShapeDtypeStruct((32, 32), f32),
+        ),
+        in_specs=[anywhere] * 2,
+        out_specs=(anywhere, anywhere),
+        scratch_shapes=[
+            pltpu.VMEM((1024, 128), f32),
+            pltpu.VMEM((32, 32), f32),
+            dma((CHUNKS + 1,)),
+            dma((CHUNKS + 1,)),
+        ],
+        compiler_params=pltpu.CompilerParams(vmem_limit_bytes=60 * 1024 * 1024),
+    )(orbitals, projected)
     return orbitals.reshape(trial_block.shape), projected
 
 

time: 60.8 us -> 59.4 us (0.977)
  local copies, waits for them, and re-layouts: 2.5 us -> 0 us
  Pallas kernels: 57.5 us -> 58.5 us
    unnamed x4 -> x0, local copies, waits for them, and re-layouts: 2.5 us -> none
    pallas_call x0 -> x1, Pallas kernels: none -> 1.81 us  [shards(): pl.pallas_call(hand_over, out_shape=(jax.ShapeDtypeStruct((1024, 128), f3...]
    pallas_call x1, Pallas kernels: 57.5 us -> 56.7 us  [shards(): pl.pallas_call(functools.partial(kernel, rings), out_shape=(jax.ShapeDtyp...]
where the time goes in v6:
time: 59.4 us; the launch traced here: 59.1 us
  Pallas kernels  58.5 us (98%)
  between operations  0.64 us (1%)
    pallas_call x1, Pallas kernels, shards(): pl.pallas_call(functools.partial(kernel, rings), out_shape=(jax.ShapeDtyp...  56.7 us
    pallas_call x1, Pallas kernels, shards(): pl.pallas_call(hand_over, out_shape=(jax.ShapeDtypeStruct((1024, 128), f3...  1.81 us

profile of v6, /device:TPU:1, one launch (start us, length us, event | category | flops | bytes accessed | tf_op | source)
XLA Modules:
  0.0 59.1 jit_solution(15564140900001449059)
XLA Ops:
  0.6 56.7 %shard_map.41 = (f32[1024,128]{1,0:T(8,128)}, f32[32,32]{1,0:T(8,128)}) custom-call(f32[1024,128]{1,0:T(8,128)} %bitcast.2, f32[8,8,128]{2,1,0:T(8,128)} %potential.1), custom_call_target="tpu_custom_call" | custom-call | flops 200000000 | bytes 1100000 | tf_op jit(solution)/shard_map/pallas_call | solution.py:620
  57.3 1.8 %shard_map.42 = (f32[1024,128]{1,0:T(8,128)}, f32[32,32]{1,0:T(8,128)}) custom-call(f32[1024,128]{1,0:T(8,128)} %get-tuple-element.6.orbitals, f32[32,32]{1,0:T(8,128)} %get-tuple-element.7.projected), custom_call_target="tpu_custom_call" | custom-call | tf_op jit(solution)/shard_map/pallas_call | solution.py:668

commit v7 on v6

--- a/solution.py
+++ b/solution.py
@@ -21,7 +21,6 @@
 PARTS = 2
 YS = 8 // PARTS
 SHIFT = (0, 8, 64, 72)
-CHUNKS = 2
 RINGS = {256: (4, 8, 8), 8: (2, 2, 2)}
 
 
@@ -518,16 +517,19 @@
     own = [jnp.where(band == 0, inverse[q], inverse[2 + q]) for q in range(2)]
     own = split_rows(jnp.concatenate([v + pltpu.roll(v, 8, 1) for v in own], 0))[:, :64]
 
-    for part in range(PARTS):
-        for x in range(8):
+    outs = []
+    for x in range(8):
+        for part in range(PARTS):
             at_x = pl.ds(128 * YS * (8 * part + x), 128 * YS)
             value = lax.dot_general(own, split[:, at_x], NN, preferred_element_type=jnp.float32)
             value = value[:16] + value[16:]
             for y in range(YS):
-                row = x * 8 + part * YS + y
-                nat[pl.ds(row, 16, stride=64), :] = value[:, 128 * y : 128 * y + 128]
-    out = pltpu.make_async_copy(nat, orbitals, in_sem.at[0])
-    out.start()
+                row = x // 4 * 512 + x % 4 * 8 + part * YS + y
+                nat[pl.ds(row, 16, stride=32), :] = value[:, 128 * y : 128 * y + 128]
+        if x % 4 == 3:
+            rows_of = pl.ds(x // 4 * 512, 512)
+            outs.append(pltpu.make_async_copy(nat.at[rows_of], orbitals.at[rows_of], in_sem.at[x // 4]))
+            outs[-1].start()
 
     dot = functools.partial(
         lax.dot_general, precision=lax.Precision.HIGHEST, preferred_element_type=jnp.float32
@@ -560,7 +562,8 @@
     two = dot(dot(inverse, image, NT), narrow, NT)
     projected[...] = 0.5 * (one + two)
 
-    out.wait()
+    for out in outs:
+        out.wait()
 
 
 def eliminated(rows, subs):
@@ -599,9 +602,8 @@
 
 def hand_over(orbitals, projected, orbitals_out, projected_out, rows, matrix, read_sem, write_sem):
     steps = [(projected, matrix, projected_out)]
-    for i in range(CHUNKS):
-        part = pl.ds(i * (1024 // CHUNKS), 1024 // CHUNKS)
-        steps.append((orbitals.at[part], rows.at[part], orbitals_out.at[part]))
+    for i in range(2):
+        steps.append((orbitals.at[i], rows.at[i], orbitals_out.at[:, pl.ds(32 * i, 32)]))
     reads = [pltpu.make_async_copy(a, b, read_sem.at[i]) for i, (a, b, _) in enumerate(steps)]
     writes = [pltpu.make_async_copy(b, c, write_sem.at[i]) for i, (_, b, c) in enumerate(steps)]
     for read in reads:
@@ -668,19 +670,19 @@
     orbitals, projected = pl.pallas_call(
         hand_over,
         out_shape=(
-            jax.ShapeDtypeStruct((1024, 128), f32),
+            jax.ShapeDtypeStruct((16, 64, 128), f32),
             jax.ShapeDtypeStruct((32, 32), f32),
         ),
         in_specs=[anywhere] * 2,
         out_specs=(anywhere, anywhere),
         scratch_shapes=[
-            pltpu.VMEM((1024, 128), f32),
+            pltpu.VMEM((2, 16, 32, 128), f32),
             pltpu.VMEM((32, 32), f32),
-            dma((CHUNKS + 1,)),
-            dma((CHUNKS + 1,)),
+            dma((3,)),
+            dma((3,)),
         ],
         compiler_params=pltpu.CompilerParams(vmem_limit_bytes=60 * 1024 * 1024),
-    )(orbitals, projected)
+    )(orbitals.reshape(2, 16, 32, 128), projected)
     return orbitals.reshape(trial_block.shape), projected
 
 

time: 59.4 us -> 59.3 us (level)
  no operation moved by 1% of the time
where the time goes in v7:
time: 59.3 us; the launch traced here: 59.1 us
  Pallas kernels  58.4 us (98%)
  between operations  0.64 us (1%)
    pallas_call x1, Pallas kernels, shards(): pl.pallas_call(functools.partial(kernel, rings), out_shape=(jax.ShapeDtyp...  56.6 us
    pallas_call x1, Pallas kernels, shards(): pl.pallas_call(hand_over, out_shape=(jax.ShapeDtypeStruct((16, 64, 128),...  1.81 us

profile of v7, /device:TPU:1, one launch (start us, length us, event | category | flops | bytes accessed | tf_op | source)
XLA Modules:
  0.0 59.1 jit_solution(837851307499469050)
XLA Ops:
  0.6 56.6 %shard_map.41 = (f32[1024,128]{1,0:T(8,128)}, f32[32,32]{1,0:T(8,128)}) custom-call(f32[1024,128]{1,0:T(8,128)} %bitcast.4, f32[8,8,128]{2,1,0:T(8,128)} %potential.1), custom_call_target="tpu_custom_call" | custom-call | flops 200000000 | bytes 1100000 | tf_op jit(solution)/shard_map/pallas_call | solution.py:622
  57.3 1.8 %shard_map.42 = (f32[16,64,128]{2,1,0:T(8,128)}, f32[32,32]{1,0:T(8,128)}) custom-call(f32[2,16,32,128]{3,2,1,0:T(8,128)} %bitcast.3, f32[32,32]{1,0:T(8,128)} %get-tuple-element.7.projected), custom_call_target="tpu_custom_call" | custom-call | tf_op jit(solution)/shard_map/pallas_call | solution.py:670
